TPU v7x, 512 devices: a whole 4x8x8 slice. The times are simulated.
512 devices in a mesh: dp: 16 (over z, core), seq: 32 (over y, x).
Axes of the slice: x: 4, y: 8, z: 8, core: 2. Of those that a mesh axis runs over, the one named last changes fastest.
Arguments:
- queries: bfloat16 [16, 4096, 2048], P('dp', 'seq'), may hold values from -110 to 110
- keys: bfloat16 [16, 4096, 512], P('dp', 'seq'), may hold values from -6 to 6
- values: bfloat16 [16, 4096, 512], P('dp', 'seq'), may hold values from -6 to 6
- grad_out: bfloat16 [16, 4096, 2048], P('dp', 'seq'), may hold values from -6 to 6
- doc_ids: int32 [16, 4096], P('dp'), may hold values from 0 to 15, never falling along the last dimension, each value on 1 to 2048 neighbouring positions
- partner_bits: int32 [16, 32], P('dp'), may hold values from 0 to 31
- q_gain: float32 [16, 128], replicated, may hold values from 0.5 to 1.5
Outputs:
- grad_queries: bfloat16 [16, 4096, 2048], P('dp', 'seq')
- grad_keys: bfloat16 [16, 4096, 512], P('dp', 'seq')
- grad_values: bfloat16 [16, 4096, 512], P('dp', 'seq')
- grad_gain: float32 [16, 128], replicated
All inputs are finite; a program needn't handle non-finite values.
Results may differ from a plain program's by a relative error of at most 0.01.
Values may be sent and summed in bfloat16 or wider, within the bound.
No kernel may reach another device: no remote copies, remote signals or barrier semaphores. Data moves between devices by JAX's collectives and lax.ppermute only.
A program may use at most 64 MiB of HBM per device.

v0:
```python
import jax
import jax.numpy as jnp
from jax import lax
from jax.sharding import PartitionSpec as P


def passed_along(value, axis, steps):
    count = lax.axis_size(axis)
    leading, last = (max(0, -steps), min(count, count - steps))
    return lax.ppermute(value, axis, [(source, source + steps) for source in range(leading, last)])


def attend(q_group, out_grad, key_group, value_group, mask, scale):
    scores = (
        jnp.einsum("brd,kd->rbk", q_group, key_group, preferred_element_type=jnp.float32) * scale
    )
    scores = jnp.where(mask[None], scores, jnp.float32(-1e30))
    top = jnp.max(scores, axis=-1, keepdims=True)
    expo = jnp.exp(scores - top)
    total = jnp.sum(expo, axis=-1, keepdims=True)
    prob = expo / total
    prob_half = prob.astype(jnp.bfloat16)
    output = jnp.einsum(
        "rbk,kd->brd", prob_half, value_group, preferred_element_type=jnp.float32
    ).astype(jnp.bfloat16)
    delta = jnp.sum(out_grad.astype(jnp.float32) * output.astype(jnp.float32), axis=-1).T
    dprob = jnp.einsum("brd,kd->rbk", out_grad, value_group, preferred_element_type=jnp.float32)
    dscore = (prob * (dprob - delta[:, :, None])).astype(jnp.bfloat16)
    dquery = (
        jnp.einsum("rbk,kd->brd", dscore, key_group, preferred_element_type=jnp.float32) * scale
    )
    log_total = top[..., 0] + jnp.log(total[..., 0])
    return (dquery, dscore, prob_half, log_total, delta)


def key_terms(dscore, prob_half, q_group, out_grad, scale):
    dkey = jnp.einsum("rbk,brd->kd", dscore, q_group, preferred_element_type=jnp.float32) * scale
    dvalue = jnp.einsum("rbk,brd->kd", prob_half, out_grad, preferred_element_type=jnp.float32)
    return (dkey, dvalue)


def key_side(q_all, grad_all, log_total, deltas, own_keys, own_values, mask, scale):
    kv_heads, hdim = (own_keys.shape[1], own_keys.shape[2])
    group = q_all.shape[1] // kv_heads
    dk_parts = []
    dv_parts = []
    for head in range(kv_heads):
        lo = head * group
        q_group = q_all[:, lo : lo + group]
        out_grad = grad_all[:, lo : lo + group]
        key_group = own_keys[:, head]
        scores = (
            jnp.einsum("brd,kd->rbk", q_group, key_group, preferred_element_type=jnp.float32)
            * scale
        )
        prob = jnp.where(
            mask[None], jnp.exp(scores - log_total[lo : lo + group, :, None]), jnp.float32(0.0)
        )
        dprob = jnp.einsum(
            "brd,kd->rbk", out_grad, own_values[:, head], preferred_element_type=jnp.float32
        )
        dscore = (prob * (dprob - deltas[lo : lo + group, :, None])).astype(jnp.bfloat16)
        dkey, dvalue = key_terms(dscore, prob.astype(jnp.bfloat16), q_group, out_grad, scale)
        dk_parts.append(dkey)
        dv_parts.append(dvalue)
    rows = own_keys.shape[0]
    return (
        jnp.stack(dk_parts, 1).reshape(rows, kv_heads * hdim),
        jnp.stack(dv_parts, 1).reshape(rows, kv_heads * hdim),
    )


def local(queries, keys, values, grad_out, doc_ids, partner_bits, q_gain):
    blk = queries.shape[1]
    heads, hdim = q_gain.shape
    kv_heads = keys.shape[2] // hdim
    group = heads // kv_heads
    scale = hdim ** (-0.5)
    count = lax.axis_size("seq")
    levels = count.bit_length() - 1
    here = lax.axis_index("seq")
    offsets = jnp.arange(blk, dtype=jnp.int32)
    docs_all = doc_ids[0]
    bits_all = partner_bits[0]
    raw = queries[0].reshape(blk, heads, hdim)
    scaled = (raw.astype(jnp.float32) * q_gain).astype(jnp.bfloat16)
    dout = grad_out[0].reshape(blk, heads, hdim)
    own_keys = keys[0]
    own_values = values[0]
    my_bits = lax.dynamic_index_in_dim(bits_all, here, 0, keepdims=False)
    query_pos = here * blk + offsets
    query_docs = lax.dynamic_slice_in_dim(docs_all, here * blk, blk, 0)

    def block_mask(source, live):
        first = jnp.maximum(source, 0) * blk
        k_docs = lax.dynamic_slice_in_dim(docs_all, first, blk, 0)
        k_pos = first + offsets
        return (
            live & (k_docs[None, :] == query_docs[:, None]) & (k_pos[None, :] <= query_pos[:, None])
        )

    key_list = [own_keys]
    value_list = [own_values]
    masks = [block_mask(here, jnp.bool_(True))]
    for level in range(levels):
        dist = 2**level
        fetched_k, fetched_v = passed_along((own_keys, own_values), "seq", dist)
        live = (my_bits // dist % 2 == 1) & (here >= dist)
        key_list.append(fetched_k)
        value_list.append(fetched_v)
        masks.append(block_mask(here - dist, live))
    all_keys = jnp.concatenate(key_list, 0).reshape(-1, kv_heads, hdim)
    all_values = jnp.concatenate(value_list, 0).reshape(-1, kv_heads, hdim)
    mask = jnp.concatenate(masks, 1)
    dq_parts, ds_parts, pb_parts, lse_parts, delta_parts = ([], [], [], [], [])
    for head in range(kv_heads):
        lo = head * group
        dquery, dscore, prob_half, log_total, delta = attend(
            scaled[:, lo : lo + group],
            dout[:, lo : lo + group],
            all_keys[:, head],
            all_values[:, head],
            mask,
            scale,
        )
        dq_parts.append(dquery)
        ds_parts.append(dscore)
        pb_parts.append(prob_half)
        lse_parts.append(log_total)
        delta_parts.append(delta)
    dquery = jnp.concatenate(dq_parts, 1)
    log_totals = jnp.concatenate(lse_parts, 0)
    deltas = jnp.concatenate(delta_parts, 0)
    own_k3 = own_keys.reshape(blk, kv_heads, hdim)
    own_v3 = own_values.reshape(blk, kv_heads, hdim)
    key_total, value_total = key_side(
        scaled, dout, log_totals, deltas, own_k3, own_v3, mask[:, :blk], scale
    )
    for level in range(levels):
        dist = 2**level
        far_q, far_grad = passed_along((scaled, dout), "seq", -dist)
        far_lse, far_delta = passed_along((log_totals, deltas), "seq", -dist)
        sender = here + dist
        clamped = jnp.minimum(sender, count - 1)
        sender_bits = lax.dynamic_index_in_dim(bits_all, clamped, 0, keepdims=False)
        live = (sender_bits // dist % 2 == 1) & (sender < count)
        sender_docs = lax.dynamic_slice_in_dim(docs_all, clamped * blk, blk, 0)
        sender_pos = sender * blk + offsets
        far_mask = (
            live
            & (query_docs[None, :] == sender_docs[:, None])
            & (query_pos[None, :] <= sender_pos[:, None])
        )
        dkey, dvalue = key_side(
            far_q, far_grad, far_lse, far_delta, own_k3, own_v3, far_mask, scale
        )
        key_total = key_total + lax.optimization_barrier(dkey.astype(jnp.bfloat16)).astype(
            jnp.float32
        )
        value_total = value_total + lax.optimization_barrier(dvalue.astype(jnp.bfloat16)).astype(
            jnp.float32
        )
    gain_term = jnp.sum(dquery * raw.astype(jnp.float32), axis=0)
    grad_gain = lax.psum(gain_term, ("dp", "seq"))
    grad_q = (dquery * q_gain).astype(jnp.bfloat16).reshape(1, blk, heads * hdim)
    return (
        grad_q,
        key_total.astype(jnp.bfloat16)[None],
        value_total.astype(jnp.bfloat16)[None],
        grad_gain,
    )


def solution(mesh):
    return jax.shard_map(
        local,
        mesh=mesh,
        in_specs=(
            P("dp", "seq", None),
            P("dp", "seq", None),
            P("dp", "seq", None),
            P("dp", "seq", None),
            P("dp", None),
            P("dp", None),
            P(),
        ),
        out_specs=(P("dp", "seq", None), P("dp", "seq", None), P("dp", "seq", None), P()),
        check_vma=False,
    )
```

profile of v0, /device:TPU:58, one launch (start us, length us, event | category | flops | bytes accessed | tf_op | source)
XLA Modules:
  0.0 451.5 jit_solution(15003509232211346737)
XLA Ops:
  1.7 3.4 collective-permute-start
  34.8 2.5 collective-permute-start.5
  48.7 2.6 fusion.543
  51.3 2.4 fusion.544
  53.7 2.4 fusion.545
  56.4 16.4 %collective-permute-start.26 = (bf16[128,16,128]{2,0,1:T(8,128)(2,1)}, bf16[128,16,128]{2,0,1:T(8,128)(2,1)}, u32[]{:S(2)}, u32[]{:S(2)}) collective-permute-start(bf16[128,16,128]{2,0,1:T(8,128)(2,1)} %multiply_convert_fusion), channel_id=1, source_target_pairs={{16,0},{17,1},{18,2},{19,3},{20,4},{21,5},{22,6},{23,7},{24,8},{25... | collective-permute-start | bytes 1572872 | tf_op jit(solution)/shard_map/ppermute | solution.py:10
  73.6 5.6 %collective-permute-start.22 = (bf16[128,16,128]{2,0,1:T(8,128)(2,1)}, bf16[128,16,128]{2,0,1:T(8,128)(2,1)}, u32[]{:S(2)}, u32[]{:S(2)}) collective-permute-start(bf16[128,16,128]{2,0,1:T(8,128)(2,1)} %multiply_convert_fusion), channel_id=1, source_target_pairs={{8,0},{9,1},{10,2},{11,3},{12,4},{13,5},{14,6},{15,7},{16,8},{17,9... | collective-permute-start | bytes 1572872 | tf_op jit(solution)/shard_map/ppermute | solution.py:10
  85.4 2.1 fusion.211
  96.9 3.0 fusion.171
  101.3 3.0 fusion.170
  105.8 3.0 fusion.169
  110.4 3.0 fusion.168
  120.8 134.0 %psum.7 = f32[16,128]{1,0:T(8,128)} all-reduce(f32[16,128]{1,0:T(8,128)S(1)} %bitcast.1469), channel_id=1, replica_groups=mesh['dp'=16,'seq'=32] {'dp','seq'}, use_global_device_ids=true, to_apply=%region_13.14 | all-reduce | flops 2048 | bytes 16384 | tf_op jit(solution)/shard_map/psum | solution.py:164
  254.8 6.7 %collective-permute-start.29 = (f32[16,128]{1,0:T(8,128)S(1)}, f32[16,128]{1,0:T(8,128)S(1)}, u32[]{:S(2)}, u32[]{:S(2)}) collective-permute-start(f32[16,128]{1,0:T(8,128)S(1)} %pad_maximum_fusion.14), channel_id=1, source_target_pairs={{16,0},{17,1},{18,2},{19,3},{20,4},{21,5},{22,6},{23,7},{24,8},{25... | collective-permute-start | bytes 24584 | tf_op jit(solution)/shard_map/ppermute | solution.py:10
  262.8 2.1 collective-permute-start.23
  266.3 8.4 %collective-permute-start.25 = (f32[16,128]{1,0:T(8,128)S(1)}, f32[16,128]{1,0:T(8,128)S(1)}, u32[]{:S(2)}, u32[]{:S(2)}) collective-permute-start(f32[16,128]{1,0:T(8,128)S(1)} %pad_maximum_fusion.14), channel_id=1, source_target_pairs={{8,0},{9,1},{10,2},{11,3},{12,4},{13,5},{14,6},{15,7},{16,8},{17,9... | collective-permute-start | bytes 24584 | tf_op jit(solution)/shard_map/ppermute | solution.py:10
  276.1 3.3 collective-permute-start.19
  280.7 5.5 %collective-permute-start.21 = (f32[16,128]{1,0:T(8,128)S(1)}, f32[16,128]{1,0:T(8,128)S(1)}, u32[]{:S(2)}, u32[]{:S(2)}) collective-permute-start(f32[16,128]{1,0:T(8,128)S(1)} %pad_maximum_fusion.14), channel_id=1, source_target_pairs={{4,0},{5,1},{6,2},{7,3},{8,4},{9,5},{10,6},{11,7},{12,8},{13,9},{1... | collective-permute-start | bytes 24584 | tf_op jit(solution)/shard_map/ppermute | solution.py:10
  287.6 4.5 collective-permute-start.15
  294.6 5.4 %collective-permute-start.17 = (f32[16,128]{1,0:T(8,128)S(1)}, f32[16,128]{1,0:T(8,128)S(1)}, u32[]{:S(2)}, u32[]{:S(2)}) collective-permute-start(f32[16,128]{1,0:T(8,128)S(1)} %pad_maximum_fusion.14), channel_id=1, source_target_pairs={{2,0},{3,1},{4,2},{5,3},{6,4},{7,5},{8,6},{9,7},{10,8},{11,9},{12,... | collective-permute-start | bytes 24584 | tf_op jit(solution)/shard_map/ppermute | solution.py:10
  301.6 2.7 collective-permute-start.11
  305.0 2.2 collective-permute-done.11
  307.2 5.2 %collective-permute-start.13 = (f32[16,128]{1,0:T(8,128)S(1)}, f32[16,128]{1,0:T(8,128)S(1)}, u32[]{:S(2)}, u32[]{:S(2)}) collective-permute-start(f32[16,128]{1,0:T(8,128)S(1)} %pad_maximum_fusion.14), channel_id=1, source_target_pairs={{1,0},{2,1},{3,2},{4,3},{5,4},{6,5},{7,6},{8,7},{9,8},{10,9},{11,1... | collective-permute-start | bytes 24584 | tf_op jit(solution)/shard_map/ppermute | solution.py:10
  313.7 5.4 %collective-permute-start.18 = (bf16[128,16,128]{2,0,1:T(8,128)(2,1)}, bf16[128,16,128]{2,0,1:T(8,128)(2,1)}, u32[]{:S(2)}, u32[]{:S(2)}) collective-permute-start(bf16[128,16,128]{2,0,1:T(8,128)(2,1)} %multiply_convert_fusion), channel_id=1, source_target_pairs={{4,0},{5,1},{6,2},{7,3},{8,4},{9,5},{10,6},{11,7},{12,8},{13,9},{1... | collective-permute-start | bytes 1572872 | tf_op jit(solution)/shard_map/ppermute | solution.py:10
  319.7 4.6 %collective-permute-start.20 = (bf16[128,16,128]{0,2,1:T(8,128)(2,1)S(1)}, bf16[128,16,128]{0,2,1:T(8,128)(2,1)S(1)}, u32[]{:S(2)}, u32[]{:S(2)}) collective-permute-start(bf16[128,16,128]{0,2,1:T(8,128)(2,1)S(1)} %bitcast.1431), channel_id=1, source_target_pairs={{4,0},{5,1},{6,2},{7,3},{8,4},{9,5},{10,6},{11,7},{12,8},{13,9},{1... | collective-permute-start | bytes 1572872 | tf_op jit(solution)/shard_map/ppermute | solution.py:10
  329.7 9.5 %collective-permute-start.14 = (bf16[128,16,128]{2,0,1:T(8,128)(2,1)}, bf16[128,16,128]{2,0,1:T(8,128)(2,1)}, u32[]{:S(2)}, u32[]{:S(2)}) collective-permute-start(bf16[128,16,128]{2,0,1:T(8,128)(2,1)} %multiply_convert_fusion), channel_id=1, source_target_pairs={{2,0},{3,1},{4,2},{5,3},{6,4},{7,5},{8,6},{9,7},{10,8},{11,9},{12,... | collective-permute-start | bytes 1572872 | tf_op jit(solution)/shard_map/ppermute | solution.py:10
  344.7 3.1 collective-permute-start.16
  357.6 7.7 %collective-permute-start.10 = (bf16[128,16,128]{2,0,1:T(8,128)(2,1)}, bf16[128,16,128]{2,0,1:T(8,128)(2,1)}, u32[]{:S(2)}, u32[]{:S(2)}) collective-permute-start(bf16[128,16,128]{2,0,1:T(8,128)(2,1)} %multiply_convert_fusion), channel_id=1, source_target_pairs={{1,0},{2,1},{3,2},{4,3},{5,4},{6,5},{7,6},{8,7},{9,8},{10,9},{11,1... | collective-permute-start | bytes 1572872 | tf_op jit(solution)/shard_map/ppermute | solution.py:10
  369.0 7.7 %collective-permute-start.12 = (bf16[128,16,128]{0,2,1:T(8,128)(2,1)S(1)}, bf16[128,16,128]{0,2,1:T(8,128)(2,1)S(1)}, u32[]{:S(2)}, u32[]{:S(2)}) collective-permute-start(bf16[128,16,128]{0,2,1:T(8,128)(2,1)S(1)} %bitcast.1433), channel_id=1, source_target_pairs={{1,0},{2,1},{3,2},{4,3},{5,4},{6,5},{7,6},{8,7},{9,8},{10,9},{11,1... | collective-permute-start | bytes 1572872 | tf_op jit(solution)/shard_map/ppermute | solution.py:10
  382.7 2.0 fusion.335
  431.9 2.0 fusion.344
  433.9 2.1 fusion.345
  (316 shorter events, 160.8 us)
Async XLA Ops:
  1.7 33.2 %collective-permute-start = (bf16[128,512]{0,1:T(8,128)(2,1)S(1)}, bf16[128,512]{0,1:T(8,128)(2,1)S(1)}, u32[]{:S(2)}, u32[]{:S(2)}) collective-permute-start(bf16[128,512]{0,1:T(8,128)(2,1)S(1)} %bitcast.1437), channel_id=1, source_target_pairs={{0,1},{1,2},{2,3},{3,4},{4,5},{5,6},{6,7},{7,8},{8,9},{9,10},{10,1... | collective-permute-start | bytes 393224 | tf_op jit(solution)/shard_map/ppermute | solution.py:10
  5.1 32.4 %collective-permute-start.1 = (bf16[128,512]{0,1:T(8,128)(2,1)S(1)}, bf16[128,512]{0,1:T(8,128)(2,1)S(1)}, u32[]{:S(2)}, u32[]{:S(2)}) collective-permute-start(bf16[128,512]{0,1:T(8,128)(2,1)S(1)} %bitcast.1438), channel_id=1, source_target_pairs={{0,2},{1,3},{2,4},{3,5},{4,6},{5,7},{6,8},{7,9},{8,10},{9,11},{10,... | collective-permute-start | bytes 393224 | tf_op jit(solution)/shard_map/ppermute | solution.py:10
  7.0 32.6 %collective-permute-start.2 = (bf16[128,512]{0,1:T(8,128)(2,1)S(1)}, bf16[128,512]{0,1:T(8,128)(2,1)S(1)}, u32[]{:S(2)}, u32[]{:S(2)}) collective-permute-start(bf16[128,512]{0,1:T(8,128)(2,1)S(1)} %bitcast.1439), channel_id=1, source_target_pairs={{0,4},{1,5},{2,6},{3,7},{4,8},{5,9},{6,10},{7,11},{8,12},{9,13},{1... | collective-permute-start | bytes 393224 | tf_op jit(solution)/shard_map/ppermute | solution.py:10
  8.3 32.7 %collective-permute-start.3 = (bf16[128,512]{0,1:T(8,128)(2,1)S(1)}, bf16[128,512]{0,1:T(8,128)(2,1)S(1)}, u32[]{:S(2)}, u32[]{:S(2)}) collective-permute-start(bf16[128,512]{0,1:T(8,128)(2,1)S(1)} %bitcast.1440), channel_id=1, source_target_pairs={{0,8},{1,9},{2,10},{3,11},{4,12},{5,13},{6,14},{7,15},{8,16},{9,17... | collective-permute-start | bytes 393224 | tf_op jit(solution)/shard_map/ppermute | solution.py:10
  9.6 32.9 %collective-permute-start.4 = (bf16[128,512]{0,1:T(8,128)(2,1)S(1)}, bf16[128,512]{0,1:T(8,128)(2,1)S(1)}, u32[]{:S(2)}, u32[]{:S(2)}) collective-permute-start(bf16[128,512]{0,1:T(8,128)(2,1)S(1)} %bitcast.1441), channel_id=1, source_target_pairs={{0,16},{1,17},{2,18},{3,19},{4,20},{5,21},{6,22},{7,23},{8,24},{9,... | collective-permute-start | bytes 393224 | tf_op jit(solution)/shard_map/ppermute | solution.py:10
  34.8 21.6 %collective-permute-start.5 = (bf16[128,512]{1,0:T(8,128)(2,1)S(1)}, bf16[128,512]{1,0:T(8,128)(2,1)S(1)}, u32[]{:S(2)}, u32[]{:S(2)}) collective-permute-start(bf16[128,512]{1,0:T(8,128)(2,1)S(1)} %bitcast.1458), channel_id=1, source_target_pairs={{0,1},{1,2},{2,3},{3,4},{4,5},{5,6},{6,7},{7,8},{8,9},{9,10},{10,1... | collective-permute-start | bytes 393224 | tf_op jit(solution)/shard_map/ppermute | solution.py:10
  37.5 36.2 %collective-permute-start.6 = (bf16[128,512]{1,0:T(8,128)(2,1)S(1)}, bf16[128,512]{1,0:T(8,128)(2,1)S(1)}, u32[]{:S(2)}, u32[]{:S(2)}) collective-permute-start(bf16[128,512]{1,0:T(8,128)(2,1)S(1)} %bitcast.1459), channel_id=1, source_target_pairs={{0,2},{1,3},{2,4},{3,5},{4,6},{5,7},{6,8},{7,9},{8,10},{9,11},{10,... | collective-permute-start | bytes 393224 | tf_op jit(solution)/shard_map/ppermute | solution.py:10
  39.6 40.5 %collective-permute-start.7 = (bf16[128,512]{1,0:T(8,128)(2,1)S(1)}, bf16[128,512]{1,0:T(8,128)(2,1)S(1)}, u32[]{:S(2)}, u32[]{:S(2)}) collective-permute-start(bf16[128,512]{1,0:T(8,128)(2,1)S(1)} %bitcast.1460), channel_id=1, source_target_pairs={{0,4},{1,5},{2,6},{3,7},{4,8},{5,9},{6,10},{7,11},{8,12},{9,13},{1... | collective-permute-start | bytes 393224 | tf_op jit(solution)/shard_map/ppermute | solution.py:10
  41.0 41.2 %collective-permute-start.8 = (bf16[128,512]{1,0:T(8,128)(2,1)S(1)}, bf16[128,512]{1,0:T(8,128)(2,1)S(1)}, u32[]{:S(2)}, u32[]{:S(2)}) collective-permute-start(bf16[128,512]{1,0:T(8,128)(2,1)S(1)} %bitcast.1461), channel_id=1, source_target_pairs={{0,8},{1,9},{2,10},{3,11},{4,12},{5,13},{6,14},{7,15},{8,16},{9,17... | collective-permute-start | bytes 393224 | tf_op jit(solution)/shard_map/ppermute | solution.py:10
  42.5 42.1 %collective-permute-start.9 = (bf16[128,512]{1,0:T(8,128)(2,1)S(1)}, bf16[128,512]{1,0:T(8,128)(2,1)S(1)}, u32[]{:S(2)}, u32[]{:S(2)}) collective-permute-start(bf16[128,512]{1,0:T(8,128)(2,1)S(1)} %bitcast.1462), channel_id=1, source_target_pairs={{0,16},{1,17},{2,18},{3,19},{4,20},{5,21},{6,22},{7,23},{8,24},{9,... | collective-permute-start | bytes 393224 | tf_op jit(solution)/shard_map/ppermute | solution.py:10
  56.4 263.2 %collective-permute-start.26 = (bf16[128,16,128]{2,0,1:T(8,128)(2,1)}, bf16[128,16,128]{2,0,1:T(8,128)(2,1)}, u32[]{:S(2)}, u32[]{:S(2)}) collective-permute-start(bf16[128,16,128]{2,0,1:T(8,128)(2,1)} %multiply_convert_fusion), channel_id=1, source_target_pairs={{16,0},{17,1},{18,2},{19,3},{20,4},{21,5},{22,6},{23,7},{24,8},{25... | collective-permute-start | bytes 1572872 | tf_op jit(solution)/shard_map/ppermute | solution.py:10
  73.6 256.1 %collective-permute-start.22 = (bf16[128,16,128]{2,0,1:T(8,128)(2,1)}, bf16[128,16,128]{2,0,1:T(8,128)(2,1)}, u32[]{:S(2)}, u32[]{:S(2)}) collective-permute-start(bf16[128,16,128]{2,0,1:T(8,128)(2,1)} %multiply_convert_fusion), channel_id=1, source_target_pairs={{8,0},{9,1},{10,2},{11,3},{12,4},{13,5},{14,6},{15,7},{16,8},{17,9... | collective-permute-start | bytes 1572872 | tf_op jit(solution)/shard_map/ppermute | solution.py:10
  80.1 264.6 %collective-permute-start.28 = (bf16[128,16,128]{0,2,1:T(8,128)(2,1)S(1)}, bf16[128,16,128]{0,2,1:T(8,128)(2,1)S(1)}, u32[]{:S(2)}, u32[]{:S(2)}) collective-permute-start(bf16[128,16,128]{0,2,1:T(8,128)(2,1)S(1)} %bitcast.1413), channel_id=1, source_target_pairs={{16,0},{17,1},{18,2},{19,3},{20,4},{21,5},{22,6},{23,7},{24,8},{25... | collective-permute-start | bytes 1572872 | tf_op jit(solution)/shard_map/ppermute | solution.py:10
  82.2 286.8 %collective-permute-start.24 = (bf16[128,16,128]{0,2,1:T(8,128)(2,1)S(1)}, bf16[128,16,128]{0,2,1:T(8,128)(2,1)S(1)}, u32[]{:S(2)}, u32[]{:S(2)}) collective-permute-start(bf16[128,16,128]{0,2,1:T(8,128)(2,1)S(1)} %bitcast.1414), channel_id=1, source_target_pairs={{8,0},{9,1},{10,2},{11,3},{12,4},{13,5},{14,6},{15,7},{16,8},{17,9... | collective-permute-start | bytes 1572872 | tf_op jit(solution)/shard_map/ppermute | solution.py:10
  114.9 139.9 %collective-permute-start.27 = (f32[16,128]{1,0:T(8,128)S(1)}, f32[16,128]{1,0:T(8,128)S(1)}, u32[]{:S(2)}, u32[]{:S(2)}) collective-permute-start(f32[16,128]{1,0:T(8,128)S(1)} %pad_maximum_fusion.13), channel_id=1, source_target_pairs={{16,0},{17,1},{18,2},{19,3},{20,4},{21,5},{22,6},{23,7},{24,8},{25... | collective-permute-start | bytes 24584 | tf_op jit(solution)/shard_map/ppermute | solution.py:10
  119.1 207.5 %copy-start.47 = (pred[128,128]{1,0:T(8,128)(4,1)S(1)}, pred[128,128]{1,0:T(8,128)(4,1)}, u32[]{:S(2)}) copy-start(pred[128,128]{1,0:T(8,128)(4,1)} %get-tuple-element.68) | copy-start | bytes 49156
  119.1 220.2 %copy-start.45 = (pred[128,128]{1,0:T(8,128)(4,1)S(1)}, pred[128,128]{1,0:T(8,128)(4,1)}, u32[]{:S(2)}) copy-start(pred[128,128]{1,0:T(8,128)(4,1)} %get-tuple-element.67) | copy-start | bytes 49156
  254.8 8.0 %collective-permute-start.29 = (f32[16,128]{1,0:T(8,128)S(1)}, f32[16,128]{1,0:T(8,128)S(1)}, u32[]{:S(2)}, u32[]{:S(2)}) collective-permute-start(f32[16,128]{1,0:T(8,128)S(1)} %pad_maximum_fusion.14), channel_id=1, source_target_pairs={{16,0},{17,1},{18,2},{19,3},{20,4},{21,5},{22,6},{23,7},{24,8},{25... | collective-permute-start | bytes 24584 | tf_op jit(solution)/shard_map/ppermute | solution.py:10
  262.8 3.5 collective-permute-start.23
  266.3 9.8 %collective-permute-start.25 = (f32[16,128]{1,0:T(8,128)S(1)}, f32[16,128]{1,0:T(8,128)S(1)}, u32[]{:S(2)}, u32[]{:S(2)}) collective-permute-start(f32[16,128]{1,0:T(8,128)S(1)} %pad_maximum_fusion.14), channel_id=1, source_target_pairs={{8,0},{9,1},{10,2},{11,3},{12,4},{13,5},{14,6},{15,7},{16,8},{17,9... | collective-permute-start | bytes 24584 | tf_op jit(solution)/shard_map/ppermute | solution.py:10
  276.1 4.7 %collective-permute-start.19 = (f32[16,128]{1,0:T(8,128)S(1)}, f32[16,128]{1,0:T(8,128)S(1)}, u32[]{:S(2)}, u32[]{:S(2)}) collective-permute-start(f32[16,128]{1,0:T(8,128)S(1)} %pad_maximum_fusion.13), channel_id=1, source_target_pairs={{4,0},{5,1},{6,2},{7,3},{8,4},{9,5},{10,6},{11,7},{12,8},{13,9},{1... | collective-permute-start | bytes 24584 | tf_op jit(solution)/shard_map/ppermute | solution.py:10
  280.7 6.8 %collective-permute-start.21 = (f32[16,128]{1,0:T(8,128)S(1)}, f32[16,128]{1,0:T(8,128)S(1)}, u32[]{:S(2)}, u32[]{:S(2)}) collective-permute-start(f32[16,128]{1,0:T(8,128)S(1)} %pad_maximum_fusion.14), channel_id=1, source_target_pairs={{4,0},{5,1},{6,2},{7,3},{8,4},{9,5},{10,6},{11,7},{12,8},{13,9},{1... | collective-permute-start | bytes 24584 | tf_op jit(solution)/shard_map/ppermute | solution.py:10
  287.6 7.0 %collective-permute-start.15 = (f32[16,128]{1,0:T(8,128)S(1)}, f32[16,128]{1,0:T(8,128)S(1)}, u32[]{:S(2)}, u32[]{:S(2)}) collective-permute-start(f32[16,128]{1,0:T(8,128)S(1)} %pad_maximum_fusion.13), channel_id=1, source_target_pairs={{2,0},{3,1},{4,2},{5,3},{6,4},{7,5},{8,6},{9,7},{10,8},{11,9},{12,... | collective-permute-start | bytes 24584 | tf_op jit(solution)/shard_map/ppermute | solution.py:10
  294.6 7.0 %collective-permute-start.17 = (f32[16,128]{1,0:T(8,128)S(1)}, f32[16,128]{1,0:T(8,128)S(1)}, u32[]{:S(2)}, u32[]{:S(2)}) collective-permute-start(f32[16,128]{1,0:T(8,128)S(1)} %pad_maximum_fusion.14), channel_id=1, source_target_pairs={{2,0},{3,1},{4,2},{5,3},{6,4},{7,5},{8,6},{9,7},{10,8},{11,9},{12,... | collective-permute-start | bytes 24584 | tf_op jit(solution)/shard_map/ppermute | solution.py:10
  301.6 5.5 %collective-permute-start.11 = (f32[16,128]{1,0:T(8,128)S(1)}, f32[16,128]{1,0:T(8,128)S(1)}, u32[]{:S(2)}, u32[]{:S(2)}) collective-permute-start(f32[16,128]{1,0:T(8,128)S(1)} %pad_maximum_fusion.13), channel_id=1, source_target_pairs={{1,0},{2,1},{3,2},{4,3},{5,4},{6,5},{7,6},{8,7},{9,8},{10,9},{11,1... | collective-permute-start | bytes 24584 | tf_op jit(solution)/shard_map/ppermute | solution.py:10
  307.2 6.5 %collective-permute-start.13 = (f32[16,128]{1,0:T(8,128)S(1)}, f32[16,128]{1,0:T(8,128)S(1)}, u32[]{:S(2)}, u32[]{:S(2)}) collective-permute-start(f32[16,128]{1,0:T(8,128)S(1)} %pad_maximum_fusion.14), channel_id=1, source_target_pairs={{1,0},{2,1},{3,2},{4,3},{5,4},{6,5},{7,6},{8,7},{9,8},{10,9},{11,1... | collective-permute-start | bytes 24584 | tf_op jit(solution)/shard_map/ppermute | solution.py:10
  313.7 43.9 %collective-permute-start.18 = (bf16[128,16,128]{2,0,1:T(8,128)(2,1)}, bf16[128,16,128]{2,0,1:T(8,128)(2,1)}, u32[]{:S(2)}, u32[]{:S(2)}) collective-permute-start(bf16[128,16,128]{2,0,1:T(8,128)(2,1)} %multiply_convert_fusion), channel_id=1, source_target_pairs={{4,0},{5,1},{6,2},{7,3},{8,4},{9,5},{10,6},{11,7},{12,8},{13,9},{1... | collective-permute-start | bytes 1572872 | tf_op jit(solution)/shard_map/ppermute | solution.py:10
  319.7 75.8 %collective-permute-start.20 = (bf16[128,16,128]{0,2,1:T(8,128)(2,1)S(1)}, bf16[128,16,128]{0,2,1:T(8,128)(2,1)S(1)}, u32[]{:S(2)}, u32[]{:S(2)}) collective-permute-start(bf16[128,16,128]{0,2,1:T(8,128)(2,1)S(1)} %bitcast.1431), channel_id=1, source_target_pairs={{4,0},{5,1},{6,2},{7,3},{8,4},{9,5},{10,6},{11,7},{12,8},{13,9},{1... | collective-permute-start | bytes 1572872 | tf_op jit(solution)/shard_map/ppermute | solution.py:10
  329.7 58.8 %collective-permute-start.14 = (bf16[128,16,128]{2,0,1:T(8,128)(2,1)}, bf16[128,16,128]{2,0,1:T(8,128)(2,1)}, u32[]{:S(2)}, u32[]{:S(2)}) collective-permute-start(bf16[128,16,128]{2,0,1:T(8,128)(2,1)} %multiply_convert_fusion), channel_id=1, source_target_pairs={{2,0},{3,1},{4,2},{5,3},{6,4},{7,5},{8,6},{9,7},{10,8},{11,9},{12,... | collective-permute-start | bytes 1572872 | tf_op jit(solution)/shard_map/ppermute | solution.py:10
  344.7 67.3 %collective-permute-start.16 = (bf16[128,16,128]{0,2,1:T(8,128)(2,1)S(1)}, bf16[128,16,128]{0,2,1:T(8,128)(2,1)S(1)}, u32[]{:S(2)}, u32[]{:S(2)}) collective-permute-start(bf16[128,16,128]{0,2,1:T(8,128)(2,1)S(1)} %bitcast.1432), channel_id=1, source_target_pairs={{2,0},{3,1},{4,2},{5,3},{6,4},{7,5},{8,6},{9,7},{10,8},{11,9},{12,... | collective-permute-start | bytes 1572872 | tf_op jit(solution)/shard_map/ppermute | solution.py:10
  357.6 50.8 %collective-permute-start.10 = (bf16[128,16,128]{2,0,1:T(8,128)(2,1)}, bf16[128,16,128]{2,0,1:T(8,128)(2,1)}, u32[]{:S(2)}, u32[]{:S(2)}) collective-permute-start(bf16[128,16,128]{2,0,1:T(8,128)(2,1)} %multiply_convert_fusion), channel_id=1, source_target_pairs={{1,0},{2,1},{3,2},{4,3},{5,4},{6,5},{7,6},{8,7},{9,8},{10,9},{11,1... | collective-permute-start | bytes 1572872 | tf_op jit(solution)/shard_map/ppermute | solution.py:10
  369.0 62.9 %collective-permute-start.12 = (bf16[128,16,128]{0,2,1:T(8,128)(2,1)S(1)}, bf16[128,16,128]{0,2,1:T(8,128)(2,1)S(1)}, u32[]{:S(2)}, u32[]{:S(2)}) collective-permute-start(bf16[128,16,128]{0,2,1:T(8,128)(2,1)S(1)} %bitcast.1433), channel_id=1, source_target_pairs={{1,0},{2,1},{3,2},{4,3},{5,4},{6,5},{7,6},{8,7},{9,8},{10,9},{11,1... | collective-permute-start | bytes 1572872 | tf_op jit(solution)/shard_map/ppermute | solution.py:10
  (51 other events, 924.1 us)
where the time goes:
time: 454 us; the launch traced here: 451 us
  blocking collectives  134 us (30%)
  starting transfers between devices  125 us (28%)
  matrix products  115 us (25%)
  local copies, waits for them, and re-layouts  35.9 us (8%)
  between operations  17.3 us (4%)
  other arithmetic  13.8 us (3%)
  waiting for transfers between devices  10.3 us (2%)
    psum x1, blocking collectives, local(): grad_gain = lax.psum(gain_term, ('dp', 'seq'))  134 us
    ppermute x30, starting transfers between devices, passed_along(): lax.ppermute(value, axis, [(source, source + steps) for source in range(l...  125 us
    dot_general x24, matrix products, key_terms(): jnp.einsum('rbk,brd->kd', dscore, q_group, preferred_element_type=jnp.flo...  45.4 us
    dot_general x24, matrix products, key_side(): jnp.einsum('brd,kd->rbk', q_group, key_group, preferred_element_type=jnp....  39.2 us
    unnamed x121, local copies, waits for them, and re-layouts  14 us
    dot_general x4, matrix products, attend(): jnp.einsum('rbk,kd->brd', dscore, key_group, preferred_element_type=jnp.f...  12 us
    ppermute x30, waiting for transfers between devices, passed_along(): lax.ppermute(value, axis, [(source, source + steps) for source in range(l...  10.3 us
  transfers between devices with their start and end apart: 30, of which 9 were waited for; matrix products, arithmetic and copies ran while one was open for 31% of the time, Pallas kernels for 0%

commit v1 on v0

v1 whole, which is shorter than its diff:
```python
import math

import jax
import jax.numpy as jnp
from jax import lax
from jax.experimental import pallas as pl
from jax.experimental.pallas import tpu as pltpu
from jax.sharding import PartitionSpec as P

HIDDEN = -1e30


def passed_along(value, axis, steps):
    count = lax.axis_size(axis)
    leading, last = (max(0, -steps), min(count, count - steps))
    return lax.ppermute(value, axis, [(source, source + steps) for source in range(leading, last)])


def summed(value, axis):
    count = lax.axis_size(axis)
    copies = jnp.broadcast_to(value[None], (count,) + value.shape)
    return jnp.sum(lax.all_to_all(copies, axis, 0, 0, tiled=True), axis=0)


def attention_kernel(levels, kv_heads, group, blk, hdim, *refs):
    here_ref, bits_ref, docs_ref, q_ref, g_ref, gain_ref, k_ref, v_ref = refs[:8]
    far_refs = refs[8 : 8 + levels]
    dq_ref, own_ref = refs[8 + levels : 10 + levels]
    term_refs = refs[10 + levels : 10 + 2 * levels]
    gg_ref = refs[10 + 2 * levels]
    bias_s, s_s, dp_s, ph_s, ds_s = refs[11 + 2 * levels :]
    scale = hdim ** (-0.5)
    here = here_ref[0]
    bits = bits_ref[0, here]
    width = group * hdim
    kv_width = kv_heads * hdim

    def doc_row(block):
        return docs_ref[0:1, pl.ds(pl.multiple_of(block * blk, blk), blk)]

    q_docs = doc_row(here)
    for level in range(levels + 1):
        dist = 0 if level == 0 else 2 ** (level - 1)
        k_docs = jnp.broadcast_to(doc_row(jnp.maximum(here - dist, 0)), (blk, blk)).T
        seen = k_docs == q_docs
        if level == 0:
            key_pos = lax.broadcasted_iota(jnp.int32, (blk, blk), 0)
            query_pos = lax.broadcasted_iota(jnp.int32, (blk, blk), 1)
            seen = seen & (key_pos <= query_pos)
            bias = jnp.where(seen, 0.0, HIDDEN)
        else:
            live = (((bits >> (level - 1)) & 1) == 1) & (here >= dist)
            bias = jnp.where(seen, jnp.where(live, 0.0, HIDDEN), HIDDEN)
        bias_s[level * blk : (level + 1) * blk, :] = bias.astype(jnp.float32)

    for head in range(kv_heads):
        lo, klo = head * width, head * hdim
        q_parts, g_parts = [], []
        for i in range(group):
            one = q_ref[0, :, lo + i * hdim : lo + (i + 1) * hdim].astype(jnp.float32)
            gain = gain_ref[head * group + i : head * group + i + 1, :]
            q_parts.append((one * gain).astype(jnp.bfloat16))
            g_parts.append(g_ref[0, :, lo + i * hdim : lo + (i + 1) * hdim])
        q_cat = jnp.concatenate(q_parts, 0)
        g_cat = jnp.concatenate(g_parts, 0)
        k_all = jnp.concatenate(
            [k_ref[0, :, klo : klo + hdim]] + [r[:, klo : klo + hdim] for r in far_refs], 0
        )
        v_all = jnp.concatenate(
            [v_ref[0, :, klo : klo + hdim]]
            + [r[:, kv_width + klo : kv_width + klo + hdim] for r in far_refs],
            0,
        )
        across = (((1,), (1,)), ((), ()))
        s_s[...] = lax.dot_general(k_all, q_cat, across, preferred_element_type=jnp.float32)
        dp_s[...] = lax.dot_general(v_all, g_cat, across, preferred_element_type=jnp.float32)
        top = None
        for level in range(levels + 1):
            rows = slice(level * blk, (level + 1) * blk)
            bias = bias_s[rows, :]
            s = s_s[rows, :] + jnp.concatenate([bias] * group, 1)
            s_s[rows, :] = s
            part = jnp.max(s, axis=0, keepdims=True)
            top = part if top is None else jnp.maximum(top, part)
        total = jnp.zeros_like(top)
        weighted = jnp.zeros_like(top)
        for level in range(levels + 1):
            rows = slice(level * blk, (level + 1) * blk)
            p = jnp.exp2((s_s[rows, :] - top) * jnp.float32(scale * math.log2(math.e)))
            s_s[rows, :] = p
            total = total + jnp.sum(p, axis=0, keepdims=True)
            weighted = weighted + jnp.sum(p * dp_s[rows, :], axis=0, keepdims=True)
        inverse = 1.0 / total
        delta = weighted * inverse
        for level in range(levels + 1):
            rows = slice(level * blk, (level + 1) * blk)
            prob = s_s[rows, :] * inverse
            ph_s[rows, :] = prob.astype(jnp.bfloat16)
            ds_s[rows, :] = (prob * (dp_s[rows, :] - delta)).astype(jnp.bfloat16)
        ds = ds_s[...]
        dk = jnp.dot(ds, q_cat, preferred_element_type=jnp.float32) * scale
        dv = jnp.dot(ph_s[...], g_cat, preferred_element_type=jnp.float32)
        own_ref[:, klo : klo + hdim] = dk[:blk]
        own_ref[:, kv_width + klo : kv_width + klo + hdim] = dv[:blk]
        for level in range(levels):
            rows = slice((level + 1) * blk, (level + 2) * blk)
            term_refs[level][:, klo : klo + hdim] = dk[rows].astype(jnp.bfloat16)
            term_refs[level][:, kv_width + klo : kv_width + klo + hdim] = dv[rows].astype(
                jnp.bfloat16
            )
        dq_t = (
            lax.dot_general(
                k_all, ds, (((0,), (0,)), ((), ())), preferred_element_type=jnp.float32
            )
            * scale
        )
        for i in range(group):
            cols = slice(lo + i * hdim, lo + (i + 1) * hdim)
            row = slice(head * group + i, head * group + i + 1)
            dq = dq_t[:, i * blk : (i + 1) * blk].T
            raw = q_ref[0, :, cols].astype(jnp.float32)
            gg_ref[row, :] = jnp.sum(dq * raw, axis=0, keepdims=True)
            dq_ref[0, :, cols] = (dq * gain_ref[row, :]).astype(jnp.bfloat16)


def attention(here, bits, docs, queries, grad_out, q_gain, keys, values, far):
    levels = len(far)
    blk = queries.shape[1]
    heads, hdim = q_gain.shape
    kv_width = keys.shape[2]
    kv_heads = kv_width // hdim
    group = heads // kv_heads
    all_rows = (levels + 1) * blk
    vmem = pl.BlockSpec(memory_space=pltpu.VMEM)
    smem = pl.BlockSpec(memory_space=pltpu.SMEM)

    def kernel(*refs):
        attention_kernel(levels, kv_heads, group, blk, hdim, *refs)

    return pl.pallas_call(
        kernel,
        out_shape=[
            jax.ShapeDtypeStruct(queries.shape, jnp.bfloat16),
            jax.ShapeDtypeStruct((blk, 2 * kv_width), jnp.float32),
        ]
        + [jax.ShapeDtypeStruct((blk, 2 * kv_width), jnp.bfloat16)] * levels
        + [jax.ShapeDtypeStruct((heads, hdim), jnp.float32)],
        in_specs=[smem, smem] + [vmem] * (6 + levels),
        out_specs=[vmem] * (3 + levels),
        scratch_shapes=[
            pltpu.VMEM((all_rows, blk), jnp.float32),
            pltpu.VMEM((all_rows, group * blk), jnp.float32),
            pltpu.VMEM((all_rows, group * blk), jnp.float32),
            pltpu.VMEM((all_rows, group * blk), jnp.bfloat16),
            pltpu.VMEM((all_rows, group * blk), jnp.bfloat16),
        ],
        compiler_params=pltpu.CompilerParams(vmem_limit_bytes=40 * 2**20),
        name="attention_both_ways",
    )(here, bits, docs, queries, grad_out, q_gain, keys, values, *far)


def local(queries, keys, values, grad_out, doc_ids, partner_bits, q_gain):
    count = lax.axis_size("seq")
    levels = count.bit_length() - 1
    here = lax.axis_index("seq")
    kv_width = keys.shape[2]
    own = jnp.concatenate([keys[0], values[0]], 1)
    far = [passed_along(own, "seq", 2**level) for level in range(levels)]
    results = attention(
        here.astype(jnp.int32)[None],
        partner_bits,
        doc_ids,
        queries,
        grad_out,
        q_gain,
        keys,
        values,
        far,
    )
    grad_q, total, terms, gain_term = results[0], results[1], results[2:-1], results[-1]
    for level in range(levels):
        total = total + passed_along(terms[level], "seq", -(2**level)).astype(jnp.float32)
    grad_gain = summed(summed(gain_term, "seq"), "dp")
    return (
        grad_q,
        total[:, :kv_width].astype(jnp.bfloat16)[None],
        total[:, kv_width:].astype(jnp.bfloat16)[None],
        grad_gain,
    )


def solution(mesh):
    return jax.shard_map(
        local,
        mesh=mesh,
        in_specs=(
            P("dp", "seq", None),
            P("dp", "seq", None),
            P("dp", "seq", None),
            P("dp", "seq", None),
            P("dp", None),
            P("dp", None),
            P(),
        ),
        out_specs=(P("dp", "seq", None), P("dp", "seq", None), P("dp", "seq", None), P()),
        check_vma=False,
    )
```

time: 454 us -> 124 us (0.27)
  the two profiles are of different devices: /device:TPU:58 before, /device:TPU:200 now
where the time goes in v1:
time: 124 us; the launch traced here: 123 us
  starting transfers between devices  55.9 us (45%)
  waiting for transfers between devices  51.1 us (41%)
  Pallas kernels  7.09 us (6%)
  local copies, waits for them, and re-layouts  6.36 us (5%)
  other arithmetic  1.93 us (2%)
    ppermute x10, waiting for transfers between devices, passed_along(): lax.ppermute(value, axis, [(source, source + steps) for source in range(l...  50.6 us
    ppermute x10, starting transfers between devices, passed_along(): lax.ppermute(value, axis, [(source, source + steps) for source in range(l...  30.8 us
    all_to_all x2, starting transfers between devices, summed(): return jnp.sum(lax.all_to_all(copies, axis, 0, 0, tiled=True), axis=0)  25.2 us
    pallas_call x1, Pallas kernels, attention(): pl.pallas_call(kernel, out_shape=[jax.ShapeDtypeStruct(queries.shape, jnp...  7.09 us
    unnamed x18, local copies, waits for them, and re-layouts  4.27 us
  transfers between devices with their start and end apart: 12, of which 8 were waited for; matrix products, arithmetic and copies ran while one was open for 1% of the time, Pallas kernels for 0%

profile of v1, /device:TPU:200, one launch (start us, length us, event | category | flops | bytes accessed | tf_op | source)
XLA Modules:
  0.0 123.2 jit_solution(7435251425637456300)
XLA Ops:
  0.7 1.0 pad_maximum_fusion
  1.7 6.8 %collective-permute-start.4 = (bf16[128,1024]{1,0:T(8,128)(2,1)S(1)}, bf16[128,1024]{1,0:T(8,128)(2,1)S(1)}, u32[]{:S(2)}, u32[]{:S(2)}) collective-permute-start(bf16[128,1024]{1,0:T(8,128)(2,1)S(1)} %pad_maximum_fusion), channel_id=1, source_target_pairs={{0,16},{1,17},{2,18},{3,19},{4,20},{5,21},{6,22},{7,23},{8,24},{9,... | collective-permute-start | bytes 786440 | tf_op jit(solution)/shard_map/ppermute | solution.py:16
  8.6 2.7 %collective-permute-start.3 = (bf16[128,1024]{1,0:T(8,128)(2,1)S(1)}, bf16[128,1024]{1,0:T(8,128)(2,1)S(1)}, u32[]{:S(2)}, u32[]{:S(2)}) collective-permute-start(bf16[128,1024]{1,0:T(8,128)(2,1)S(1)} %pad_maximum_fusion), channel_id=1, source_target_pairs={{0,8},{1,9},{2,10},{3,11},{4,12},{5,13},{6,14},{7,15},{8,16},{9,17... | collective-permute-start | bytes 786440 | tf_op jit(solution)/shard_map/ppermute | solution.py:16
  11.3 1.9 %collective-permute-start.2 = (bf16[128,1024]{1,0:T(8,128)(2,1)S(1)}, bf16[128,1024]{1,0:T(8,128)(2,1)S(1)}, u32[]{:S(2)}, u32[]{:S(2)}) collective-permute-start(bf16[128,1024]{1,0:T(8,128)(2,1)S(1)} %pad_maximum_fusion), channel_id=1, source_target_pairs={{0,4},{1,5},{2,6},{3,7},{4,8},{5,9},{6,10},{7,11},{8,12},{9,13},{1... | collective-permute-start | bytes 786440 | tf_op jit(solution)/shard_map/ppermute | solution.py:16
  13.2 4.9 %collective-permute-start.1 = (bf16[128,1024]{1,0:T(8,128)(2,1)S(1)}, bf16[128,1024]{1,0:T(8,128)(2,1)S(1)}, u32[]{:S(2)}, u32[]{:S(2)}) collective-permute-start(bf16[128,1024]{1,0:T(8,128)(2,1)S(1)} %pad_maximum_fusion), channel_id=1, source_target_pairs={{0,2},{1,3},{2,4},{3,5},{4,6},{5,7},{6,8},{7,9},{8,10},{9,11},{10,... | collective-permute-start | bytes 786440 | tf_op jit(solution)/shard_map/ppermute | solution.py:16
  18.1 2.5 %collective-permute-start = (bf16[128,1024]{1,0:T(8,128)(2,1)S(1)}, bf16[128,1024]{1,0:T(8,128)(2,1)S(1)}, u32[]{:S(2)}, u32[]{:S(2)}) collective-permute-start(bf16[128,1024]{1,0:T(8,128)(2,1)S(1)} %pad_maximum_fusion), channel_id=1, source_target_pairs={{0,1},{1,2},{2,3},{3,4},{4,5},{5,6},{6,7},{7,8},{8,9},{9,10},{10,1... | collective-permute-start | bytes 786440 | tf_op jit(solution)/shard_map/ppermute | solution.py:16
  20.7 5.7 %collective-permute-done.3.refs_11_ = bf16[128,1024]{1,0:T(8,128)(2,1)S(1)} collective-permute-done((bf16[128,1024]{1,0:T(8,128)(2,1)S(1)}, bf16[128,1024]{1,0:T(8,128)(2,1)S(1)}, u32[]{:S(2)}, u32[]{:S(2)}) %collective-permute-start.3) | collective-permute-done | bytes 262176 | tf_op jit(solution)/shard_map/ppermute | solution.py:16
  26.3 5.5 %collective-permute-done.2.refs_10_ = bf16[128,1024]{1,0:T(8,128)(2,1)S(1)} collective-permute-done((bf16[128,1024]{1,0:T(8,128)(2,1)S(1)}, bf16[128,1024]{1,0:T(8,128)(2,1)S(1)}, u32[]{:S(2)}, u32[]{:S(2)}) %collective-permute-start.2) | collective-permute-done | bytes 262176 | tf_op jit(solution)/shard_map/ppermute | solution.py:16
  31.9 4.2 %collective-permute-done.1.refs_9_ = bf16[128,1024]{1,0:T(8,128)(2,1)S(1)} collective-permute-done((bf16[128,1024]{1,0:T(8,128)(2,1)S(1)}, bf16[128,1024]{1,0:T(8,128)(2,1)S(1)}, u32[]{:S(2)}, u32[]{:S(2)}) %collective-permute-start.1) | collective-permute-done | bytes 262176 | tf_op jit(solution)/shard_map/ppermute | solution.py:16
  36.1 4.9 %collective-permute-done.refs_8_ = bf16[128,1024]{1,0:T(8,128)(2,1)S(1)} collective-permute-done((bf16[128,1024]{1,0:T(8,128)(2,1)S(1)}, bf16[128,1024]{1,0:T(8,128)(2,1)S(1)}, u32[]{:S(2)}, u32[]{:S(2)}) %collective-permute-start) | collective-permute-done | bytes 262176 | tf_op jit(solution)/shard_map/ppermute | solution.py:16
  41.0 1.0 copy-done.1
  42.0 0.9 copy-done.2
  42.9 0.9 copy-done.3
  43.8 0.7 copy-done.4
  44.5 7.1 %attention_both_ways.1 = (bf16[1,128,2048]{2,1,0:T(8,128)(2,1)}, f32[128,1024]{1,0:T(8,128)S(1)}, bf16[128,1024]{1,0:T(8,128)(2,1)S(1)}, bf16[128,1024]{1,0:T(8,...) custom-call(s32[1]{0:T(128)} %bitcast.refs_0_, ...), custom_call_target="tpu_custom_call" | custom-call | tf_op jit(solution)/shard_map/attention_both_ways/pallas_call | solution.py:140
  51.6 0.7 copy-done.7
  52.3 0.7 broadcast_in_dim.24
  53.0 17.0 %all-to-all-start = ((f32[32,16,128]{2,1,0:T(8,128)}), f32[32,16,128]{2,1,0:T(8,128)S(1)}, u32[]{:S(2)}, u32[]{:S(2)}) async-start(f32[32,16,128]{2,1,0:T(8,128)} %broadcast_in_dim.24), calls=%async_computation | async-start | bytes 524288 | tf_op jit(solution)/shard_map/all_to_all | solution.py:22
  70.1 4.6 %collective-permute-start.5 = (bf16[128,1024]{1,0:T(8,128)(2,1)S(1)}, bf16[128,1024]{1,0:T(8,128)(2,1)S(1)}, u32[]{:S(2)}, u32[]{:S(2)}) collective-permute-start(bf16[128,1024]{1,0:T(8,128)(2,1)S(1)} %copy-done.8), channel_id=1, source_target_pairs={{1,0},{2,1},{3,2},{4,3},{5,4},{6,5},{7,6},{8,7},{9,8},{10,9},{11,1... | collective-permute-start | bytes 786440 | tf_op jit(solution)/shard_map/ppermute | solution.py:16
  74.7 2.8 %collective-permute-start.6 = (bf16[128,1024]{1,0:T(8,128)(2,1)S(1)}, bf16[128,1024]{1,0:T(8,128)(2,1)S(1)}, u32[]{:S(2)}, u32[]{:S(2)}) collective-permute-start(bf16[128,1024]{1,0:T(8,128)(2,1)S(1)} %get-tuple-element.15), channel_id=1, source_target_pairs={{2,0},{3,1},{4,2},{5,3},{6,4},{7,5},{8,6},{9,7},{10,8},{11,9},{12,... | collective-permute-start | bytes 786440 | tf_op jit(solution)/shard_map/ppermute | solution.py:16
  77.4 1.9 %collective-permute-start.7 = (bf16[128,1024]{1,0:T(8,128)(2,1)S(1)}, bf16[128,1024]{1,0:T(8,128)(2,1)S(1)}, u32[]{:S(2)}, u32[]{:S(2)}) collective-permute-start(bf16[128,1024]{1,0:T(8,128)(2,1)S(1)} %get-tuple-element.16), channel_id=1, source_target_pairs={{4,0},{5,1},{6,2},{7,3},{8,4},{9,5},{10,6},{11,7},{12,8},{13,9},{1... | collective-permute-start | bytes 786440 | tf_op jit(solution)/shard_map/ppermute | solution.py:16
  79.4 1.3 %collective-permute-start.8 = (bf16[128,1024]{1,0:T(8,128)(2,1)S(1)}, bf16[128,1024]{1,0:T(8,128)(2,1)S(1)}, u32[]{:S(2)}, u32[]{:S(2)}) collective-permute-start(bf16[128,1024]{1,0:T(8,128)(2,1)S(1)} %get-tuple-element.17), channel_id=1, source_target_pairs={{8,0},{9,1},{10,2},{11,3},{12,4},{13,5},{14,6},{15,7},{16,8},{17,9... | collective-permute-start | bytes 786440 | tf_op jit(solution)/shard_map/ppermute | solution.py:16
  80.7 1.3 %collective-permute-start.9 = (bf16[128,1024]{1,0:T(8,128)(2,1)S(1)}, bf16[128,1024]{1,0:T(8,128)(2,1)S(1)}, u32[]{:S(2)}, u32[]{:S(2)}) collective-permute-start(bf16[128,1024]{1,0:T(8,128)(2,1)S(1)} %get-tuple-element.18), channel_id=1, source_target_pairs={{16,0},{17,1},{18,2},{19,3},{20,4},{21,5},{22,6},{23,7},{24,8},{25... | collective-permute-start | bytes 786440 | tf_op jit(solution)/shard_map/ppermute | solution.py:16
  82.0 0.5 all-to-all-done
  82.5 0.7 broadcast_in_dim.25
  83.2 8.2 %all-to-all-start.1 = ((f32[16,16,128]{2,1,0:T(8,128)}), f32[16,16,128]{2,1,0:T(8,128)S(1)}, u32[]{:S(2)}, u32[]{:S(2)}) async-start(f32[16,16,128]{2,1,0:T(8,128)} %broadcast_in_dim.25), calls=%async_computation.1 | async-start | bytes 262144 | tf_op jit(solution)/shard_map/all_to_all | solution.py:22
  91.4 6.5 %collective-permute-done.7 = bf16[128,1024]{1,0:T(8,128)(2,1)S(1)} collective-permute-done((bf16[128,1024]{1,0:T(8,128)(2,1)S(1)}, bf16[128,1024]{1,0:T(8,128)(2,1)S(1)}, u32[]{:S(2)}, u32[]{:S(2)}) %collective-permute-start.7) | collective-permute-done | bytes 262176 | tf_op jit(solution)/shard_map/ppermute | solution.py:16
  97.9 6.2 %collective-permute-done.8 = bf16[128,1024]{1,0:T(8,128)(2,1)S(1)} collective-permute-done((bf16[128,1024]{1,0:T(8,128)(2,1)S(1)}, bf16[128,1024]{1,0:T(8,128)(2,1)S(1)}, u32[]{:S(2)}, u32[]{:S(2)}) %collective-permute-start.8) | collective-permute-done | bytes 262176 | tf_op jit(solution)/shard_map/ppermute | solution.py:16
  104.1 17.5 %collective-permute-done.9 = bf16[128,1024]{1,0:T(8,128)(2,1)S(1)} collective-permute-done((bf16[128,1024]{1,0:T(8,128)(2,1)S(1)}, bf16[128,1024]{1,0:T(8,128)(2,1)S(1)}, u32[]{:S(2)}, u32[]{:S(2)}) %collective-permute-start.9) | collective-permute-done | bytes 262176 | tf_op jit(solution)/shard_map/ppermute | solution.py:16
  121.7 0.2 add_convert_fusion
  121.9 0.7 slice_bitcast_fusion
  122.6 0.6 reduce_sum.19
  (18 shorter events, 0.1 us)
Async XLA Ops:
  0.6 40.3 %copy-start = (bf16[1,128,2048]{2,1,0:T(8,128)(2,1)S(1)}, bf16[1,128,2048]{2,1,0:T(8,128)(2,1)}, u32[]{:S(2)}) copy-start(bf16[1,128,2048]{2,1,0:T(8,128)(2,1)} %refs_3_.1) | copy-start | bytes 1572868
  0.6 40.3 %copy-start.5 = (f32[16,128]{1,0:T(8,128)S(1)}, f32[16,128]{1,0:T(8,128)}, u32[]{:S(2)}) copy-start(f32[16,128]{1,0:T(8,128)} %refs_5_.1) | copy-start | bytes 24580
  1.7 19.0 %collective-permute-start.4 = (bf16[128,1024]{1,0:T(8,128)(2,1)S(1)}, bf16[128,1024]{1,0:T(8,128)(2,1)S(1)}, u32[]{:S(2)}, u32[]{:S(2)}) collective-permute-start(bf16[128,1024]{1,0:T(8,128)(2,1)S(1)} %pad_maximum_fusion), channel_id=1, source_target_pairs={{0,16},{1,17},{2,18},{3,19},{4,20},{5,21},{6,22},{7,23},{8,24},{9,... | collective-permute-start | bytes 786440 | tf_op jit(solution)/shard_map/ppermute | solution.py:16
  8.6 17.8 %collective-permute-start.3 = (bf16[128,1024]{1,0:T(8,128)(2,1)S(1)}, bf16[128,1024]{1,0:T(8,128)(2,1)S(1)}, u32[]{:S(2)}, u32[]{:S(2)}) collective-permute-start(bf16[128,1024]{1,0:T(8,128)(2,1)S(1)} %pad_maximum_fusion), channel_id=1, source_target_pairs={{0,8},{1,9},{2,10},{3,11},{4,12},{5,13},{6,14},{7,15},{8,16},{9,17... | collective-permute-start | bytes 786440 | tf_op jit(solution)/shard_map/ppermute | solution.py:16
  11.3 20.6 %collective-permute-start.2 = (bf16[128,1024]{1,0:T(8,128)(2,1)S(1)}, bf16[128,1024]{1,0:T(8,128)(2,1)S(1)}, u32[]{:S(2)}, u32[]{:S(2)}) collective-permute-start(bf16[128,1024]{1,0:T(8,128)(2,1)S(1)} %pad_maximum_fusion), channel_id=1, source_target_pairs={{0,4},{1,5},{2,6},{3,7},{4,8},{5,9},{6,10},{7,11},{8,12},{9,13},{1... | collective-permute-start | bytes 786440 | tf_op jit(solution)/shard_map/ppermute | solution.py:16
  13.2 22.9 %collective-permute-start.1 = (bf16[128,1024]{1,0:T(8,128)(2,1)S(1)}, bf16[128,1024]{1,0:T(8,128)(2,1)S(1)}, u32[]{:S(2)}, u32[]{:S(2)}) collective-permute-start(bf16[128,1024]{1,0:T(8,128)(2,1)S(1)} %pad_maximum_fusion), channel_id=1, source_target_pairs={{0,2},{1,3},{2,4},{3,5},{4,6},{5,7},{6,8},{7,9},{8,10},{9,11},{10,... | collective-permute-start | bytes 786440 | tf_op jit(solution)/shard_map/ppermute | solution.py:16
  18.1 22.8 %collective-permute-start = (bf16[128,1024]{1,0:T(8,128)(2,1)S(1)}, bf16[128,1024]{1,0:T(8,128)(2,1)S(1)}, u32[]{:S(2)}, u32[]{:S(2)}) collective-permute-start(bf16[128,1024]{1,0:T(8,128)(2,1)S(1)} %pad_maximum_fusion), channel_id=1, source_target_pairs={{0,1},{1,2},{2,3},{3,4},{4,5},{5,6},{6,7},{7,8},{8,9},{9,10},{10,1... | collective-permute-start | bytes 786440 | tf_op jit(solution)/shard_map/ppermute | solution.py:16
  20.7 20.3 %copy-start.6 = (s32[1,32]{1,0:T(1,128)S(1)}, s32[1,32]{1,0:T(1,128)}, u32[]{:S(2)}) copy-start(s32[1,32]{1,0:T(1,128)} %refs_1_.1) | copy-start | bytes 388
  41.0 1.0 copy-start.1
  42.0 0.9 copy-start.2
  42.9 0.9 copy-start.3
  43.8 0.7 copy-start.4
  51.6 0.7 copy-start.7
  53.0 17.0 %copy-start.8 = (bf16[128,1024]{1,0:T(8,128)(2,1)S(1)}, bf16[128,1024]{1,0:T(8,128)(2,1)}, u32[]{:S(2)}) copy-start(bf16[128,1024]{1,0:T(8,128)(2,1)} %copy-done.7) | copy-start | bytes 786436
  53.0 29.5 %all-to-all-start = ((f32[32,16,128]{2,1,0:T(8,128)}), f32[32,16,128]{2,1,0:T(8,128)S(1)}, u32[]{:S(2)}, u32[]{:S(2)}) async-start(f32[32,16,128]{2,1,0:T(8,128)} %broadcast_in_dim.24), calls=%async_computation | async-start | bytes 524288 | tf_op jit(solution)/shard_map/all_to_all | solution.py:22
  70.1 21.3 %collective-permute-start.5 = (bf16[128,1024]{1,0:T(8,128)(2,1)S(1)}, bf16[128,1024]{1,0:T(8,128)(2,1)S(1)}, u32[]{:S(2)}, u32[]{:S(2)}) collective-permute-start(bf16[128,1024]{1,0:T(8,128)(2,1)S(1)} %copy-done.8), channel_id=1, source_target_pairs={{1,0},{2,1},{3,2},{4,3},{5,4},{6,5},{7,6},{8,7},{9,8},{10,9},{11,1... | collective-permute-start | bytes 786440 | tf_op jit(solution)/shard_map/ppermute | solution.py:16
  74.7 16.7 %collective-permute-start.6 = (bf16[128,1024]{1,0:T(8,128)(2,1)S(1)}, bf16[128,1024]{1,0:T(8,128)(2,1)S(1)}, u32[]{:S(2)}, u32[]{:S(2)}) collective-permute-start(bf16[128,1024]{1,0:T(8,128)(2,1)S(1)} %get-tuple-element.15), channel_id=1, source_target_pairs={{2,0},{3,1},{4,2},{5,3},{6,4},{7,5},{8,6},{9,7},{10,8},{11,9},{12,... | collective-permute-start | bytes 786440 | tf_op jit(solution)/shard_map/ppermute | solution.py:16
  77.4 20.5 %collective-permute-start.7 = (bf16[128,1024]{1,0:T(8,128)(2,1)S(1)}, bf16[128,1024]{1,0:T(8,128)(2,1)S(1)}, u32[]{:S(2)}, u32[]{:S(2)}) collective-permute-start(bf16[128,1024]{1,0:T(8,128)(2,1)S(1)} %get-tuple-element.16), channel_id=1, source_target_pairs={{4,0},{5,1},{6,2},{7,3},{8,4},{9,5},{10,6},{11,7},{12,8},{13,9},{1... | collective-permute-start | bytes 786440 | tf_op jit(solution)/shard_map/ppermute | solution.py:16
  79.4 24.8 %collective-permute-start.8 = (bf16[128,1024]{1,0:T(8,128)(2,1)S(1)}, bf16[128,1024]{1,0:T(8,128)(2,1)S(1)}, u32[]{:S(2)}, u32[]{:S(2)}) collective-permute-start(bf16[128,1024]{1,0:T(8,128)(2,1)S(1)} %get-tuple-element.17), channel_id=1, source_target_pairs={{8,0},{9,1},{10,2},{11,3},{12,4},{13,5},{14,6},{15,7},{16,8},{17,9... | collective-permute-start | bytes 786440 | tf_op jit(solution)/shard_map/ppermute | solution.py:16
  80.7 41.0 %collective-permute-start.9 = (bf16[128,1024]{1,0:T(8,128)(2,1)S(1)}, bf16[128,1024]{1,0:T(8,128)(2,1)S(1)}, u32[]{:S(2)}, u32[]{:S(2)}) collective-permute-start(bf16[128,1024]{1,0:T(8,128)(2,1)S(1)} %get-tuple-element.18), channel_id=1, source_target_pairs={{16,0},{17,1},{18,2},{19,3},{20,4},{21,5},{22,6},{23,7},{24,8},{25... | collective-permute-start | bytes 786440 | tf_op jit(solution)/shard_map/ppermute | solution.py:16
  83.2 39.4 %all-to-all-start.1 = ((f32[16,16,128]{2,1,0:T(8,128)}), f32[16,16,128]{2,1,0:T(8,128)S(1)}, u32[]{:S(2)}, u32[]{:S(2)}) async-start(f32[16,16,128]{2,1,0:T(8,128)} %broadcast_in_dim.25), calls=%async_computation.1 | async-start | bytes 262144 | tf_op jit(solution)/shard_map/all_to_all | solution.py:22

commit v2 on v1

v2 whole, which is shorter than its diff:
```python
import math

import jax
import jax.numpy as jnp
from jax import lax
from jax.experimental import pallas as pl
from jax.experimental.pallas import tpu as pltpu
from jax.sharding import PartitionSpec as P

HIDDEN = -1e30
ROW = 4
ACROSS = (((1,), (1,)), ((), ()))
VMEM = pl.BlockSpec(memory_space=pltpu.VMEM)
SMEM = pl.BlockSpec(memory_space=pltpu.SMEM)


def passed_along(value, steps):
    count = lax.axis_size("seq")
    leading, last = (max(0, -steps), min(count, count - steps))
    return lax.ppermute(value, "seq", [(source, source + steps) for source in range(leading, last)])


def passed_in_row(value, steps):
    count = lax.axis_size("seq")
    pairs = [(b, b // ROW * ROW + (b + steps) % ROW) for b in range(count)]
    return lax.ppermute(value, "seq", pairs)


def passed_between_rows(value, row, rows, step):
    count = lax.axis_size("seq")

    def branch(first):
        pairs = [
            (first * ROW + x, (first + step) * ROW + x)
            for x in range(ROW)
            if 0 <= (first + step) * ROW < count
        ]
        return lambda block: lax.ppermute(block, "seq", pairs)

    return lax.switch(row, [jnp.zeros_like] + [branch(first) for first in rows], value)


def summed(value, axis):
    count = lax.axis_size(axis)
    copies = jnp.broadcast_to(value[None], (count,) + value.shape)
    return jnp.sum(lax.all_to_all(copies, axis, 0, 0, tiled=True), axis=0)


def prepare_kernel(levels, kv_heads, group, blk, hdim, *refs):
    here_ref, bits_ref, docs_ref, q_ref, g_ref, gain_ref, own_ref = refs[:7]
    bias_ref, q_out, g_out, s_ref, dp_ref = refs[7:]
    here = here_ref[0]
    bits = bits_ref[0, here]
    kv_width = kv_heads * hdim

    for head in range(kv_heads):
        base = head * group * blk
        for i in range(group):
            cols = slice((head * group + i) * hdim, (head * group + i + 1) * hdim)
            rows = slice(base + i * blk, base + (i + 1) * blk)
            gain = gain_ref[head * group + i : head * group + i + 1, :]
            q_out[rows, :] = (q_ref[0, :, cols].astype(jnp.float32) * gain).astype(jnp.bfloat16)
            g_out[rows, :] = g_ref[0, :, cols]
        rows = slice(base, base + group * blk)
        out = slice(head * blk, (head + 1) * blk)
        k_own = own_ref[:, head * hdim : (head + 1) * hdim]
        v_own = own_ref[:, kv_width + head * hdim : kv_width + (head + 1) * hdim]
        s_ref[out, :] = lax.dot_general(
            k_own, q_out[rows, :], ACROSS, preferred_element_type=jnp.float32
        )
        dp_ref[out, :] = lax.dot_general(
            v_own, g_out[rows, :], ACROSS, preferred_element_type=jnp.float32
        )

    def doc_row(block):
        return docs_ref[0:1, pl.ds(pl.multiple_of(block * blk, blk), blk)]

    q_docs = doc_row(here)
    for level in range(levels + 1):
        dist = 0 if level == 0 else 2 ** (level - 1)
        k_docs = jnp.broadcast_to(doc_row(jnp.maximum(here - dist, 0)), (blk, blk)).T
        seen = k_docs == q_docs
        if level == 0:
            key_pos = lax.broadcasted_iota(jnp.int32, (blk, blk), 0)
            query_pos = lax.broadcasted_iota(jnp.int32, (blk, blk), 1)
            bias = jnp.where(seen & (key_pos <= query_pos), 0.0, HIDDEN)
        else:
            live = (((bits >> (level - 1)) & 1) == 1) & (here >= dist)
            bias = jnp.where(seen, jnp.where(live, 0.0, HIDDEN), HIDDEN)
        bias_ref[level * blk : (level + 1) * blk, :] = bias.astype(jnp.float32)


def attention_kernel(levels, kv_heads, group, blk, hdim, *refs):
    q_ref, gain_ref, bias_ref, qc_ref, gc_ref, s_ref, dp_ref, own_ref = refs[:8]
    far_refs = refs[8 : 8 + levels]
    dq_ref, sum_ref = refs[8 + levels : 10 + levels]
    term_refs = refs[10 + levels : 10 + 2 * levels]
    gg_ref = refs[10 + 2 * levels]
    s_s, dp_s, ph_s, ds_s = refs[11 + 2 * levels :]
    scale = hdim ** (-0.5)
    width = group * hdim
    kv_width = kv_heads * hdim

    for head in range(kv_heads):
        lo, klo = head * width, head * hdim
        kcols = slice(klo, klo + hdim)
        vcols = slice(kv_width + klo, kv_width + klo + hdim)
        q_cat = qc_ref[head * group * blk : (head + 1) * group * blk, :]
        g_cat = gc_ref[head * group * blk : (head + 1) * group * blk, :]
        k_far = jnp.concatenate([r[:, kcols] for r in far_refs], 0)
        v_far = jnp.concatenate([r[:, vcols] for r in far_refs], 0)
        s_s[blk:, :] = lax.dot_general(k_far, q_cat, ACROSS, preferred_element_type=jnp.float32)
        dp_s[blk:, :] = lax.dot_general(v_far, g_cat, ACROSS, preferred_element_type=jnp.float32)
        here = slice(head * blk, (head + 1) * blk)
        top = None
        for level in range(levels + 1):
            rows = slice(level * blk, (level + 1) * blk)
            s = s_ref[here, :] if level == 0 else s_s[rows, :]
            s = s + jnp.concatenate([bias_ref[rows, :]] * group, 1)
            s_s[rows, :] = s
            part = jnp.max(s, axis=0, keepdims=True)
            top = part if top is None else jnp.maximum(top, part)
        total = jnp.zeros_like(top)
        weighted = jnp.zeros_like(top)
        for level in range(levels + 1):
            rows = slice(level * blk, (level + 1) * blk)
            p = jnp.exp2((s_s[rows, :] - top) * jnp.float32(scale * math.log2(math.e)))
            s_s[rows, :] = p
            dp = dp_ref[here, :] if level == 0 else dp_s[rows, :]
            total = total + jnp.sum(p, axis=0, keepdims=True)
            weighted = weighted + jnp.sum(p * dp, axis=0, keepdims=True)
        inverse = 1.0 / total
        delta = weighted * inverse
        for level in range(levels + 1):
            rows = slice(level * blk, (level + 1) * blk)
            prob = s_s[rows, :] * inverse
            ph_s[rows, :] = prob.astype(jnp.bfloat16)
            dp = dp_ref[here, :] if level == 0 else dp_s[rows, :]
            ds_s[rows, :] = (prob * (dp - delta)).astype(jnp.bfloat16)
        ds = ds_s[...]
        dk = jnp.dot(ds, q_cat, preferred_element_type=jnp.float32) * scale
        dv = jnp.dot(ph_s[...], g_cat, preferred_element_type=jnp.float32)
        sum_ref[:, kcols] = dk[:blk]
        sum_ref[:, vcols] = dv[:blk]
        for level in range(levels):
            rows = slice((level + 1) * blk, (level + 2) * blk)
            term_refs[level][:, kcols] = dk[rows].astype(jnp.bfloat16)
            term_refs[level][:, vcols] = dv[rows].astype(jnp.bfloat16)
        k_all = jnp.concatenate([own_ref[:, kcols], k_far], 0)
        dq_t = (
            lax.dot_general(
                k_all, ds, (((0,), (0,)), ((), ())), preferred_element_type=jnp.float32
            )
            * scale
        )
        for i in range(group):
            cols = slice(lo + i * hdim, lo + (i + 1) * hdim)
            row = slice(head * group + i, head * group + i + 1)
            dq = dq_t[:, i * blk : (i + 1) * blk].T
            raw = q_ref[0, :, cols].astype(jnp.float32)
            gg_ref[row, :] = jnp.sum(dq * raw, axis=0, keepdims=True)
            dq_ref[0, :, cols] = (dq * gain_ref[row, :]).astype(jnp.bfloat16)


def local(queries, keys, values, grad_out, doc_ids, partner_bits, q_gain):
    f32, bf16 = jnp.float32, jnp.bfloat16
    count = lax.axis_size("seq")
    levels = count.bit_length() - 1
    here = lax.axis_index("seq").astype(jnp.int32)
    column = here % ROW
    blk = queries.shape[1]
    heads, hdim = q_gain.shape
    kv_width = keys.shape[2]
    kv_heads = kv_width // hdim
    group = heads // kv_heads
    sizes = (levels, kv_heads, group, blk, hdim)
    all_rows = (levels + 1) * blk

    def shape(rows, columns, dtype):
        return jax.ShapeDtypeStruct((rows, columns), dtype)

    half = count // 2 // ROW
    by_block = doc_ids[0].reshape(count, blk)
    shared = by_block[: count // 2, blk - 1] == by_block[count // 2 :, 0]
    wanted = (partner_bits[0, count // 2 :] >> (levels - 1)) & 1 == 1
    far_rows = jnp.arange(count // 2, dtype=jnp.int32) // ROW + 1
    far_row = jnp.max(jnp.where(shared & wanted, far_rows, 0))

    own = jnp.concatenate([keys[0], values[0]], 1)
    by4 = passed_along(own, 4)
    by8 = passed_along(own, 8)
    by2 = passed_along(own, 2)
    by1 = passed_in_row(jnp.where(column >= ROW - 1, by4, own), 1)
    by16 = passed_between_rows(own, far_row, range(half), half)
    far = [by1, by2, by4, by8, by16]

    bias, q_cat, g_cat, s_own, dp_own = pl.pallas_call(
        lambda *refs: prepare_kernel(*sizes, *refs),
        out_shape=[
            shape(all_rows, blk, f32),
            shape(heads * blk, hdim, bf16),
            shape(heads * blk, hdim, bf16),
            shape(kv_heads * blk, group * blk, f32),
            shape(kv_heads * blk, group * blk, f32),
        ],
        in_specs=[SMEM, SMEM] + [VMEM] * 5,
        out_specs=[VMEM] * 5,
        compiler_params=pltpu.CompilerParams(vmem_limit_bytes=40 * 2**20),
        cost_estimate=pl.CostEstimate(flops=10**9, bytes_accessed=4 * 10**6, transcendentals=0),
        name="prepare",
    )(here[None], partner_bits, doc_ids, queries, grad_out, q_gain, own)

    results = pl.pallas_call(
        lambda *refs: attention_kernel(*sizes, *refs),
        out_shape=[
            jax.ShapeDtypeStruct(queries.shape, bf16),
            shape(blk, 2 * kv_width, f32),
        ]
        + [shape(blk, 2 * kv_width, bf16)] * levels
        + [shape(heads, hdim, f32)],
        in_specs=[VMEM] * (8 + levels),
        out_specs=[VMEM] * (3 + levels),
        scratch_shapes=[
            pltpu.VMEM((all_rows, group * blk), f32),
            pltpu.VMEM((all_rows, group * blk), f32),
            pltpu.VMEM((all_rows, group * blk), bf16),
            pltpu.VMEM((all_rows, group * blk), bf16),
        ],
        compiler_params=pltpu.CompilerParams(vmem_limit_bytes=40 * 2**20),
        cost_estimate=pl.CostEstimate(
            flops=2 * 10**9, bytes_accessed=6 * 10**6, transcendentals=10**6
        ),
        name="attention_both_ways",
    )(queries, q_gain, bias, q_cat, g_cat, s_own, dp_own, own, *far)
    grad_q, total, terms, gain_term = results[0], results[1], results[2:-1], results[-1]

    back = [passed_along(terms[level], -(2**level)) for level in range(levels - 1)]
    copies = jnp.broadcast_to(gain_term[None], (count,) + gain_term.shape)
    gain_term = jnp.sum(lax.all_to_all(copies, "seq", 0, 0, tiled=True), axis=0)
    gain_term, far_term = lax.optimization_barrier((gain_term, terms[-1]))
    back.append(passed_between_rows(far_term, far_row, range(half, 2 * half), -half))
    for block in back:
        total = total + block.astype(f32)
    grad_gain = summed(gain_term, "dp")
    return (
        grad_q,
        total[:, :kv_width].astype(bf16)[None],
        total[:, kv_width:].astype(bf16)[None],
        grad_gain,
    )


def solution(mesh):
    return jax.shard_map(
        local,
        mesh=mesh,
        in_specs=(
            P("dp", "seq", None),
            P("dp", "seq", None),
            P("dp", "seq", None),
            P("dp", "seq", None),
            P("dp", None),
            P("dp", None),
            P(),
        ),
        out_specs=(P("dp", "seq", None), P("dp", "seq", None), P("dp", "seq", None), P()),
        check_vma=False,
    )
```

time: 124 us -> 92.9 us (0.75)
  the two profiles are of different devices: /device:TPU:200 before, /device:TPU:400 now
where the time goes in v2:
time: 92.9 us; the launch traced here: 92.3 us
  starting transfers between devices  46 us (50%)
  waiting for transfers between devices  27.7 us (30%)
  Pallas kernels  8.43 us (9%)
  other arithmetic  4.61 us (5%)
  local copies, waits for them, and re-layouts  4.02 us (4%)
  between operations  1.5 us (2%)
    ppermute x7, waiting for transfers between devices, passed_along(): lax.ppermute(value, 'seq', [(source, source + steps) for source in range(...  25.2 us
    ppermute x7, starting transfers between devices, passed_along(): lax.ppermute(value, 'seq', [(source, source + steps) for source in range(...  25 us
    all_to_all x1, starting transfers between devices, local(): gain_term = jnp.sum(lax.all_to_all(copies, 'seq', 0, 0, tiled=True), axis=0)  9.04 us
    all_to_all x1, starting transfers between devices, summed(): return jnp.sum(lax.all_to_all(copies, axis, 0, 0, tiled=True), axis=0)  8.59 us
    pallas_call x1, Pallas kernels, local(): pl.pallas_call(lambda *refs: attention_kernel(*sizes, *refs), out_shape=[...  7.43 us
    ppermute x1, starting transfers between devices, passed_in_row(): return lax.ppermute(value, 'seq', pairs)  3.4 us
    ppermute x1, waiting for transfers between devices, passed_in_row(): return lax.ppermute(value, 'seq', pairs)  2.44 us
  transfers between devices with their start and end apart: 10, of which 5 were waited for; matrix products, arithmetic and copies ran while one was open for 6% of the time, Pallas kernels for 1%

profile of v2, /device:TPU:400, one launch (start us, length us, event | category | flops | bytes accessed | tf_op | source)
XLA Modules:
  0.0 92.3 jit_solution(7678252312268964730)
XLA Ops:
  0.6 1.0 %pad_maximum_fusion.refs_6_.refs_7_ = bf16[128,1024]{1,0:T(8,128)(2,1)S(1)} fusion(bf16[128,512]{1,0:T(8,128)(2,1)} %bitcast.19, bf16[128,512]{1,0:T(8,128)(2,1)} %bitcast.21), kind=kLoop, calls=%fused_computation.1 | loop fusion | flops 524288 | bytes 524288 | tf_op jit(solution)/shard_map/concatenate | solution.py:189
  1.7 3.5 %collective-permute-start.8 = (bf16[128,1024]{1,0:T(8,128)(2,1)S(1)}, bf16[128,1024]{1,0:T(8,128)(2,1)S(1)}, u32[]{:S(2)}, u32[]{:S(2)}) collective-permute-start(bf16[128,1024]{1,0:T(8,128)(2,1)S(1)} %pad_maximum_fusion.refs_6_.refs_7_), channel_id=1, source_target_pairs={{0,4},{1,5},{2,6},{3,7},{4,8},{5,9},{6,10},{7,11},{8,12},{9,13},{1... | collective-permute-start | bytes 786440 | tf_op jit(solution)/shard_map/ppermute | solution.py:20
  5.2 4.8 %collective-permute-start.11 = (bf16[128,1024]{1,0:T(8,128)(2,1)S(1)}, bf16[128,1024]{1,0:T(8,128)(2,1)S(1)}, u32[]{:S(2)}, u32[]{:S(2)}) collective-permute-start(bf16[128,1024]{1,0:T(8,128)(2,1)S(1)} %pad_maximum_fusion.refs_6_.refs_7_), channel_id=1, source_target_pairs={{0,8},{1,9},{2,10},{3,11},{4,12},{5,13},{6,14},{7,15},{8,16},{9,17... | collective-permute-start | bytes 786440 | tf_op jit(solution)/shard_map/ppermute | solution.py:20
  10.0 4.9 %collective-permute-start.10 = (bf16[128,1024]{1,0:T(8,128)(2,1)S(1)}, bf16[128,1024]{1,0:T(8,128)(2,1)S(1)}, u32[]{:S(2)}, u32[]{:S(2)}) collective-permute-start(bf16[128,1024]{1,0:T(8,128)(2,1)S(1)} %pad_maximum_fusion.refs_6_.refs_7_), channel_id=1, source_target_pairs={{0,2},{1,3},{2,4},{3,5},{4,6},{5,7},{6,8},{7,9},{8,10},{9,11},{10,... | collective-permute-start | bytes 786440 | tf_op jit(solution)/shard_map/ppermute | solution.py:20
  15.0 2.9 %collective-permute-done.8.refs_10_ = bf16[128,1024]{1,0:T(8,128)(2,1)S(1)} collective-permute-done((bf16[128,1024]{1,0:T(8,128)(2,1)S(1)}, bf16[128,1024]{1,0:T(8,128)(2,1)S(1)}, u32[]{:S(2)}, u32[]{:S(2)}) %collective-permute-start.8) | collective-permute-done | bytes 262176 | tf_op jit(solution)/shard_map/ppermute | solution.py:20
  17.9 1.0 %broadcast_select_fusion = bf16[128,1024]{1,0:T(8,128)(2,1)S(1)} fusion(bf16[128,1024]{1,0:T(8,128)(2,1)S(1)} %collective-permute-done.8.refs_10_, pred[]{:T(512)S(6)} %ge.3, bf16[128,512]{1,0:T(8,128)(2,1)} %bitcast.20, bf16[128,512]{1,0:T(8,128)(2,1)} %bitcast.22), kind=kLoop, calls=%fused_computation.2 | loop fusion | flops 655360 | bytes 786433 | tf_op jit(solution)/shard_map/jit(_where)/select_n | solution.py:193
  18.9 3.4 %collective-permute-start.9 = (bf16[128,1024]{1,0:T(8,128)(2,1)S(1)}, bf16[128,1024]{1,0:T(8,128)(2,1)S(1)}, u32[]{:S(2)}, u32[]{:S(2)}) collective-permute-start(bf16[128,1024]{1,0:T(8,128)(2,1)S(1)} %broadcast_select_fusion), channel_id=1, source_target_pairs={{0,1},{1,2},{2,3},{3,0},{4,5},{5,6},{6,7},{7,4},{8,9},{9,10},{10,1... | collective-permute-start | bytes 786440 | tf_op jit(solution)/shard_map/ppermute | solution.py:26
  22.4 0.1 fusion.3
  22.4 0.1 copy.16
  22.5 0.1 copy.15
  22.6 0.6 copy-done.1
  23.2 0.7 fusion.2
  24.5 0.7 conditional.2
  24.6 0.7 broadcast.32
  25.3 1.0 %prepare.1 = (f32[768,128]{1,0:T(8,128)S(1)}, bf16[2048,128]{1,0:T(8,128)(2,1)S(1)}, bf16[2048,128]{1,0:T(8,128)(2,1)S(1)}, f32[512,512]{1,0:T(8,128)S(1)}, f32[512,512]{1,0:T(8,128)S(1)}) custom-call(s32[1]{0:T(128)} %bitcast.refs_0_, s32[1,32]{1,0:T(1,128)S(1)} %copy-done.1, s32[1,4096]{1,0:T(1,128)S(1)} %copy-done, bf16[1,128,2048]{2,1,0:T(8,128)(2,1)S(1)} %copy-done.3, ...), custom_call_target="tpu_custom_call" | custom-call | flops 1000000000 | bytes 4000000 | tf_op jit(solution)/shard_map/prepare/pallas_call | solution.py:197
  26.3 4.8 %collective-permute-done.10.refs_9_ = bf16[128,1024]{1,0:T(8,128)(2,1)S(1)} collective-permute-done((bf16[128,1024]{1,0:T(8,128)(2,1)S(1)}, bf16[128,1024]{1,0:T(8,128)(2,1)S(1)}, u32[]{:S(2)}, u32[]{:S(2)}) %collective-permute-start.10) | collective-permute-done | bytes 262176 | tf_op jit(solution)/shard_map/ppermute | solution.py:20
  31.2 2.4 %collective-permute-done.9.refs_8_ = bf16[128,1024]{1,0:T(8,128)(2,1)S(1)} collective-permute-done((bf16[128,1024]{1,0:T(8,128)(2,1)S(1)}, bf16[128,1024]{1,0:T(8,128)(2,1)S(1)}, u32[]{:S(2)}, u32[]{:S(2)}) %collective-permute-start.9) | collective-permute-done | bytes 262176 | tf_op jit(solution)/shard_map/ppermute | solution.py:26
  33.6 7.4 %attention_both_ways.1 = (bf16[1,128,2048]{2,1,0:T(8,128)(2,1)}, f32[128,1024]{1,0:T(8,128)S(1)}, bf16[128,1024]{1,0:T(8,128)(2,1)S(1)}, bf16[128,1024]{1,0:T(8,...) custom-call(bf16[1,128,2048]{2,1,0:T(8,128)(2,1)S(1)} %copy-done.3, ...), custom_call_target="tpu_custom_call" | custom-call | flops 2000000000 | bytes 6000000 | tf_op jit(solution)/shard_map/attention_both_ways/pallas_call | solution.py:213
  41.0 0.7 broadcast_in_dim.24
  41.7 9.0 %all-to-all-start = ((f32[32,16,128]{2,1,0:T(8,128)}), f32[32,16,128]{2,1,0:T(8,128)S(1)}, u32[]{:S(2)}, u32[]{:S(2)}) async-start(f32[32,16,128]{2,1,0:T(8,128)} %broadcast_in_dim.24), calls=%async_computation | async-start | bytes 524288 | tf_op jit(solution)/shard_map/all_to_all | solution.py:239
  50.8 4.6 %collective-permute-start.12 = (bf16[128,1024]{1,0:T(8,128)(2,1)S(1)}, bf16[128,1024]{1,0:T(8,128)(2,1)S(1)}, u32[]{:S(2)}, u32[]{:S(2)}) collective-permute-start(bf16[128,1024]{1,0:T(8,128)(2,1)S(1)} %get-tuple-element.47), channel_id=1, source_target_pairs={{1,0},{2,1},{3,2},{4,3},{5,4},{6,5},{7,6},{8,7},{9,8},{10,9},{11,1... | collective-permute-start | bytes 786440 | tf_op jit(solution)/shard_map/ppermute | solution.py:20
  55.4 2.8 %collective-permute-start.13 = (bf16[128,1024]{1,0:T(8,128)(2,1)S(1)}, bf16[128,1024]{1,0:T(8,128)(2,1)S(1)}, u32[]{:S(2)}, u32[]{:S(2)}) collective-permute-start(bf16[128,1024]{1,0:T(8,128)(2,1)S(1)} %get-tuple-element.48), channel_id=1, source_target_pairs={{2,0},{3,1},{4,2},{5,3},{6,4},{7,5},{8,6},{9,7},{10,8},{11,9},{12,... | collective-permute-start | bytes 786440 | tf_op jit(solution)/shard_map/ppermute | solution.py:20
  58.1 2.5 %collective-permute-start.14 = (bf16[128,1024]{1,0:T(8,128)(2,1)S(1)}, bf16[128,1024]{1,0:T(8,128)(2,1)S(1)}, u32[]{:S(2)}, u32[]{:S(2)}) collective-permute-start(bf16[128,1024]{1,0:T(8,128)(2,1)S(1)} %get-tuple-element.49), channel_id=1, source_target_pairs={{4,0},{5,1},{6,2},{7,3},{8,4},{9,5},{10,6},{11,7},{12,8},{13,9},{1... | collective-permute-start | bytes 786440 | tf_op jit(solution)/shard_map/ppermute | solution.py:20
  60.6 1.9 %collective-permute-start.15 = (bf16[128,1024]{1,0:T(8,128)(2,1)S(1)}, bf16[128,1024]{1,0:T(8,128)(2,1)}, u32[]{:S(2)}, u32[]{:S(2)}) collective-permute-start(bf16[128,1024]{1,0:T(8,128)(2,1)S(1)} %get-tuple-element.50), channel_id=1, source_target_pairs={{8,0},{9,1},{10,2},{11,3},{12,4},{13,5},{14,6},{15,7},{16,8},{17,9... | collective-permute-start | bytes 786440 | tf_op jit(solution)/shard_map/ppermute | solution.py:20
  62.6 0.7 broadcast_in_dim.27
  63.3 0.3 copy-done.5
  63.6 8.6 %all-to-all-start.1 = ((f32[16,16,128]{2,1,0:T(8,128)}), f32[16,16,128]{2,1,0:T(8,128)S(1)}, u32[]{:S(2)}, u32[]{:S(2)}) async-start(f32[16,16,128]{2,1,0:T(8,128)} %broadcast_in_dim.27), calls=%async_computation.1 | async-start | bytes 262144 | tf_op jit(solution)/shard_map/all_to_all | solution.py:46
  72.3 5.9 %collective-permute-done.14 = bf16[128,1024]{1,0:T(8,128)(2,1)S(1)} collective-permute-done((bf16[128,1024]{1,0:T(8,128)(2,1)S(1)}, bf16[128,1024]{1,0:T(8,128)(2,1)S(1)}, u32[]{:S(2)}, u32[]{:S(2)}) %collective-permute-start.14) | collective-permute-done | bytes 262176 | tf_op jit(solution)/shard_map/ppermute | solution.py:20
  78.2 11.6 %collective-permute-done.15 = bf16[128,1024]{1,0:T(8,128)(2,1)} collective-permute-done((bf16[128,1024]{1,0:T(8,128)(2,1)S(1)}, bf16[128,1024]{1,0:T(8,128)(2,1)}, u32[]{:S(2)}, u32[]{:S(2)}) %collective-permute-start.15) | collective-permute-done | bytes 262176 | tf_op jit(solution)/shard_map/ppermute | solution.py:20
  89.7 1.2 %add_convert_fusion = bf16[128,1024]{1,0:T(8,128)(2,1)S(1)} fusion(f32[128,1024]{1,0:T(8,128)S(1)} %get-tuple-element.60, bf16[128,1024]{1,0:T(8,128)(2,1)} %collective-permute-done.15, bf16[128,1024]{1,0:T(8,128)(2,1)S(1)} %collective-permute-done.14, bf16[128,1024]{1,0:T(8,128)(2,1)S(1)} %collective-permute-done.13, f32[128,1024]{1,0:T(8,128)S(1)} %get-tuple-element.46, ...), kind=kLoop, calls=%fused_computation | loop fusion | flops 1310720 | bytes 2359296 | tf_op jit(solution)/shard_map/convert.1
  90.9 0.7 slice_bitcast_fusion
  91.6 0.6 reduce_sum.19
  (18 shorter events, 0.2 us)
Async XLA Ops:
  0.6 24.7 %copy-start.3 = (bf16[1,128,2048]{2,1,0:T(8,128)(2,1)S(1)}, bf16[1,128,2048]{2,1,0:T(8,128)(2,1)}, u32[]{:S(2)}) copy-start(bf16[1,128,2048]{2,1,0:T(8,128)(2,1)} %refs_0_.1) | copy-start | bytes 1572868
  1.7 16.2 %collective-permute-start.8 = (bf16[128,1024]{1,0:T(8,128)(2,1)S(1)}, bf16[128,1024]{1,0:T(8,128)(2,1)S(1)}, u32[]{:S(2)}, u32[]{:S(2)}) collective-permute-start(bf16[128,1024]{1,0:T(8,128)(2,1)S(1)} %pad_maximum_fusion.refs_6_.refs_7_), channel_id=1, source_target_pairs={{0,4},{1,5},{2,6},{3,7},{4,8},{5,9},{6,10},{7,11},{8,12},{9,13},{1... | collective-permute-start | bytes 786440 | tf_op jit(solution)/shard_map/ppermute | solution.py:20
  5.2 21.1 %collective-permute-start.11 = (bf16[128,1024]{1,0:T(8,128)(2,1)S(1)}, bf16[128,1024]{1,0:T(8,128)(2,1)S(1)}, u32[]{:S(2)}, u32[]{:S(2)}) collective-permute-start(bf16[128,1024]{1,0:T(8,128)(2,1)S(1)} %pad_maximum_fusion.refs_6_.refs_7_), channel_id=1, source_target_pairs={{0,8},{1,9},{2,10},{3,11},{4,12},{5,13},{6,14},{7,15},{8,16},{9,17... | collective-permute-start | bytes 786440 | tf_op jit(solution)/shard_map/ppermute | solution.py:20
  10.0 21.2 %collective-permute-start.10 = (bf16[128,1024]{1,0:T(8,128)(2,1)S(1)}, bf16[128,1024]{1,0:T(8,128)(2,1)S(1)}, u32[]{:S(2)}, u32[]{:S(2)}) collective-permute-start(bf16[128,1024]{1,0:T(8,128)(2,1)S(1)} %pad_maximum_fusion.refs_6_.refs_7_), channel_id=1, source_target_pairs={{0,2},{1,3},{2,4},{3,5},{4,6},{5,7},{6,8},{7,9},{8,10},{9,11},{10,... | collective-permute-start | bytes 786440 | tf_op jit(solution)/shard_map/ppermute | solution.py:20
  15.0 7.4 %copy-start = (s32[1,4096]{1,0:T(1,128)S(1)}, s32[1,4096]{1,0:T(1,128)}, u32[]{:S(2)}) copy-start(s32[1,4096]{1,0:T(1,128)} %refs_2_.1) | copy-start | bytes 49156
  15.0 10.3 %copy-start.2 = (bf16[1,128,2048]{2,1,0:T(8,128)(2,1)S(1)}, bf16[1,128,2048]{2,1,0:T(8,128)(2,1)}, u32[]{:S(2)}) copy-start(bf16[1,128,2048]{2,1,0:T(8,128)(2,1)} %refs_4_.1) | copy-start | bytes 1572868
  18.9 14.7 %collective-permute-start.9 = (bf16[128,1024]{1,0:T(8,128)(2,1)S(1)}, bf16[128,1024]{1,0:T(8,128)(2,1)S(1)}, u32[]{:S(2)}, u32[]{:S(2)}) collective-permute-start(bf16[128,1024]{1,0:T(8,128)(2,1)S(1)} %broadcast_select_fusion), channel_id=1, source_target_pairs={{0,1},{1,2},{2,3},{3,0},{4,5},{5,6},{6,7},{7,4},{8,9},{9,10},{10,1... | collective-permute-start | bytes 786440 | tf_op jit(solution)/shard_map/ppermute | solution.py:26
  22.5 0.7 copy-start.1
  24.5 0.8 copy-start.4
  41.7 20.8 %all-to-all-start = ((f32[32,16,128]{2,1,0:T(8,128)}), f32[32,16,128]{2,1,0:T(8,128)S(1)}, u32[]{:S(2)}, u32[]{:S(2)}) async-start(f32[32,16,128]{2,1,0:T(8,128)} %broadcast_in_dim.24), calls=%async_computation | async-start | bytes 524288 | tf_op jit(solution)/shard_map/all_to_all | solution.py:239
  50.8 21.5 %collective-permute-start.12 = (bf16[128,1024]{1,0:T(8,128)(2,1)S(1)}, bf16[128,1024]{1,0:T(8,128)(2,1)S(1)}, u32[]{:S(2)}, u32[]{:S(2)}) collective-permute-start(bf16[128,1024]{1,0:T(8,128)(2,1)S(1)} %get-tuple-element.47), channel_id=1, source_target_pairs={{1,0},{2,1},{3,2},{4,3},{5,4},{6,5},{7,6},{8,7},{9,8},{10,9},{11,1... | collective-permute-start | bytes 786440 | tf_op jit(solution)/shard_map/ppermute | solution.py:20
  55.4 16.9 %collective-permute-start.13 = (bf16[128,1024]{1,0:T(8,128)(2,1)S(1)}, bf16[128,1024]{1,0:T(8,128)(2,1)S(1)}, u32[]{:S(2)}, u32[]{:S(2)}) collective-permute-start(bf16[128,1024]{1,0:T(8,128)(2,1)S(1)} %get-tuple-element.48), channel_id=1, source_target_pairs={{2,0},{3,1},{4,2},{5,3},{6,4},{7,5},{8,6},{9,7},{10,8},{11,9},{12,... | collective-permute-start | bytes 786440 | tf_op jit(solution)/shard_map/ppermute | solution.py:20
  58.1 20.0 %collective-permute-start.14 = (bf16[128,1024]{1,0:T(8,128)(2,1)S(1)}, bf16[128,1024]{1,0:T(8,128)(2,1)S(1)}, u32[]{:S(2)}, u32[]{:S(2)}) collective-permute-start(bf16[128,1024]{1,0:T(8,128)(2,1)S(1)} %get-tuple-element.49), channel_id=1, source_target_pairs={{4,0},{5,1},{6,2},{7,3},{8,4},{9,5},{10,6},{11,7},{12,8},{13,9},{1... | collective-permute-start | bytes 786440 | tf_op jit(solution)/shard_map/ppermute | solution.py:20
  60.6 29.1 %collective-permute-start.15 = (bf16[128,1024]{1,0:T(8,128)(2,1)S(1)}, bf16[128,1024]{1,0:T(8,128)(2,1)}, u32[]{:S(2)}, u32[]{:S(2)}) collective-permute-start(bf16[128,1024]{1,0:T(8,128)(2,1)S(1)} %get-tuple-element.50), channel_id=1, source_target_pairs={{8,0},{9,1},{10,2},{11,3},{12,4},{13,5},{14,6},{15,7},{16,8},{17,9... | collective-permute-start | bytes 786440 | tf_op jit(solution)/shard_map/ppermute | solution.py:20
  62.6 1.0 %copy-start.5 = (bf16[128,1024]{1,0:T(8,128)(2,1)S(1)}, bf16[128,1024]{1,0:T(8,128)(2,1)}, u32[]{:S(2)}) copy-start(bf16[128,1024]{1,0:T(8,128)(2,1)} %get-tuple-element.53) | copy-start | bytes 786436
  63.6 28.0 %all-to-all-start.1 = ((f32[16,16,128]{2,1,0:T(8,128)}), f32[16,16,128]{2,1,0:T(8,128)S(1)}, u32[]{:S(2)}, u32[]{:S(2)}) async-start(f32[16,16,128]{2,1,0:T(8,128)} %broadcast_in_dim.27), calls=%async_computation.1 | async-start | bytes 262144 | tf_op jit(solution)/shard_map/all_to_all | solution.py:46

commit v3 on v2

--- a/solution.py
+++ b/solution.py
@@ -51,7 +51,6 @@
     bias_ref, q_out, g_out, s_ref, dp_ref = refs[7:]
     here = here_ref[0]
     bits = bits_ref[0, here]
-    kv_width = kv_heads * hdim
 
     for head in range(kv_heads):
         base = head * group * blk
@@ -63,8 +62,8 @@
             g_out[rows, :] = g_ref[0, :, cols]
         rows = slice(base, base + group * blk)
         out = slice(head * blk, (head + 1) * blk)
-        k_own = own_ref[:, head * hdim : (head + 1) * hdim]
-        v_own = own_ref[:, kv_width + head * hdim : kv_width + (head + 1) * hdim]
+        k_own = own_ref[0, :, head * hdim : (head + 1) * hdim]
+        v_own = own_ref[1, :, head * hdim : (head + 1) * hdim]
         s_ref[out, :] = lax.dot_general(
             k_own, q_out[rows, :], ACROSS, preferred_element_type=jnp.float32
         )
@@ -96,21 +95,36 @@
     dq_ref, sum_ref = refs[8 + levels : 10 + levels]
     term_refs = refs[10 + levels : 10 + 2 * levels]
     gg_ref = refs[10 + 2 * levels]
-    s_s, dp_s, ph_s, ds_s = refs[11 + 2 * levels :]
+    s_s, dp_s, ph_s, ds_s, last_ref, sem = refs[11 + 2 * levels :]
+    near_refs = far_refs[:-1]
+    last = levels * blk
+    copy = pltpu.make_async_copy(far_refs[-1], last_ref, sem)
+    copy.start()
     scale = hdim ** (-0.5)
     width = group * hdim
-    kv_width = kv_heads * hdim
 
     for head in range(kv_heads):
         lo, klo = head * width, head * hdim
         kcols = slice(klo, klo + hdim)
-        vcols = slice(kv_width + klo, kv_width + klo + hdim)
         q_cat = qc_ref[head * group * blk : (head + 1) * group * blk, :]
         g_cat = gc_ref[head * group * blk : (head + 1) * group * blk, :]
-        k_far = jnp.concatenate([r[:, kcols] for r in far_refs], 0)
-        v_far = jnp.concatenate([r[:, vcols] for r in far_refs], 0)
-        s_s[blk:, :] = lax.dot_general(k_far, q_cat, ACROSS, preferred_element_type=jnp.float32)
-        dp_s[blk:, :] = lax.dot_general(v_far, g_cat, ACROSS, preferred_element_type=jnp.float32)
+        k_near = jnp.concatenate([r[0, :, kcols] for r in near_refs], 0)
+        v_near = jnp.concatenate([r[1, :, kcols] for r in near_refs], 0)
+        s_s[blk:last, :] = lax.dot_general(
+            k_near, q_cat, ACROSS, preferred_element_type=jnp.float32
+        )
+        dp_s[blk:last, :] = lax.dot_general(
+            v_near, g_cat, ACROSS, preferred_element_type=jnp.float32
+        )
+        if head == 0:
+            copy.wait()
+        k_last = last_ref[0, :, kcols]
+        s_s[last:, :] = lax.dot_general(
+            k_last, q_cat, ACROSS, preferred_element_type=jnp.float32
+        )
+        dp_s[last:, :] = lax.dot_general(
+            last_ref[1, :, kcols], g_cat, ACROSS, preferred_element_type=jnp.float32
+        )
         here = slice(head * blk, (head + 1) * blk)
         top = None
         for level in range(levels + 1):
@@ -140,13 +154,13 @@
         ds = ds_s[...]
         dk = jnp.dot(ds, q_cat, preferred_element_type=jnp.float32) * scale
         dv = jnp.dot(ph_s[...], g_cat, preferred_element_type=jnp.float32)
-        sum_ref[:, kcols] = dk[:blk]
-        sum_ref[:, vcols] = dv[:blk]
+        sum_ref[0, :, kcols] = dk[:blk]
+        sum_ref[1, :, kcols] = dv[:blk]
         for level in range(levels):
             rows = slice((level + 1) * blk, (level + 2) * blk)
-            term_refs[level][:, kcols] = dk[rows].astype(jnp.bfloat16)
-            term_refs[level][:, vcols] = dv[rows].astype(jnp.bfloat16)
-        k_all = jnp.concatenate([own_ref[:, kcols], k_far], 0)
+            term_refs[level][0, :, kcols] = dk[rows].astype(jnp.bfloat16)
+            term_refs[level][1, :, kcols] = dv[rows].astype(jnp.bfloat16)
+        k_all = jnp.concatenate([own_ref[0, :, kcols], k_near, k_last], 0)
         dq_t = (
             lax.dot_general(
                 k_all, ds, (((0,), (0,)), ((), ())), preferred_element_type=jnp.float32
@@ -186,7 +200,7 @@
     far_rows = jnp.arange(count // 2, dtype=jnp.int32) // ROW + 1
     far_row = jnp.max(jnp.where(shared & wanted, far_rows, 0))
 
-    own = jnp.concatenate([keys[0], values[0]], 1)
+    own = jnp.stack([keys[0], values[0]])
     by4 = passed_along(own, 4)
     by8 = passed_along(own, 8)
     by2 = passed_along(own, 2)
@@ -214,17 +228,19 @@
         lambda *refs: attention_kernel(*sizes, *refs),
         out_shape=[
             jax.ShapeDtypeStruct(queries.shape, bf16),
-            shape(blk, 2 * kv_width, f32),
+            jax.ShapeDtypeStruct((2, blk, kv_width), f32),
         ]
-        + [shape(blk, 2 * kv_width, bf16)] * levels
+        + [jax.ShapeDtypeStruct((2, blk, kv_width), bf16)] * levels
         + [shape(heads, hdim, f32)],
-        in_specs=[VMEM] * (8 + levels),
+        in_specs=[VMEM] * (7 + levels) + [pl.BlockSpec(memory_space=pl.ANY)],
         out_specs=[VMEM] * (3 + levels),
         scratch_shapes=[
             pltpu.VMEM((all_rows, group * blk), f32),
             pltpu.VMEM((all_rows, group * blk), f32),
             pltpu.VMEM((all_rows, group * blk), bf16),
             pltpu.VMEM((all_rows, group * blk), bf16),
+            pltpu.VMEM((2, blk, kv_width), bf16),
+            pltpu.SemaphoreType.DMA,
         ],
         compiler_params=pltpu.CompilerParams(vmem_limit_bytes=40 * 2**20),
         cost_estimate=pl.CostEstimate(
@@ -238,14 +254,15 @@
     copies = jnp.broadcast_to(gain_term[None], (count,) + gain_term.shape)
     gain_term = jnp.sum(lax.all_to_all(copies, "seq", 0, 0, tiled=True), axis=0)
     gain_term, far_term = lax.optimization_barrier((gain_term, terms[-1]))
-    back.append(passed_between_rows(far_term, far_row, range(half, 2 * half), -half))
+    back16 = passed_between_rows(far_term, far_row, range(half, 2 * half), -half)
+    back.append(jnp.where(far_row > 0, back16, 0))
     for block in back:
         total = total + block.astype(f32)
     grad_gain = summed(gain_term, "dp")
     return (
         grad_q,
-        total[:, :kv_width].astype(bf16)[None],
-        total[:, kv_width:].astype(bf16)[None],
+        total[:1].astype(bf16),
+        total[1:].astype(bf16),
         grad_gain,
     )
 

time: 92.9 us -> 95.4 us (1.027)
  the two profiles are of different devices: /device:TPU:400 before, /device:TPU:200 now
where the time goes in v3:
time: 95.4 us; the launch traced here: 94.8 us
  starting transfers between devices  55.2 us (58%)
  waiting for transfers between devices  21.8 us (23%)
  Pallas kernels  8.76 us (9%)
  local copies, waits for them, and re-layouts  4.24 us (4%)
  other arithmetic  2.57 us (3%)
  between operations  2.16 us (2%)
    ppermute x7, starting transfers between devices, passed_along(): lax.ppermute(value, 'seq', [(source, source + steps) for source in range(...  24.8 us
    ppermute x2, waiting for transfers between devices, branch(): return lambda block: lax.ppermute(block, 'seq', pairs)  20.1 us
    all_to_all x1, starting transfers between devices, local(): gain_term = jnp.sum(lax.all_to_all(copies, 'seq', 0, 0, tiled=True), axis=0)  11.3 us
    all_to_all x1, starting transfers between devices, summed(): return jnp.sum(lax.all_to_all(copies, axis, 0, 0, tiled=True), axis=0)  10.9 us
    pallas_call x1, Pallas kernels, local(): pl.pallas_call(lambda *refs: attention_kernel(*sizes, *refs), out_shape=[...  7.75 us
    ppermute x2, starting transfers between devices, branch(): return lambda block: lax.ppermute(block, 'seq', pairs)  4.76 us
    ppermute x1, starting transfers between devices, passed_in_row(): return lax.ppermute(value, 'seq', pairs)  3.4 us
    unnamed x17, local copies, waits for them, and re-layouts  2.05 us
  transfers between devices with their start and end apart: 12, of which 4 were waited for; matrix products, arithmetic and copies ran while one was open for 4% of the time, Pallas kernels for 1%

profile of v3, /device:TPU:200, one launch (start us, length us, event | category | flops | bytes accessed | tf_op | source)
XLA Modules:
  0.0 94.8 jit_solution(3596079076824817388)
XLA Ops:
  0.6 0.9 %constant_dynamic-update-slice_fusion.1 = bf16[2,128,512]{2,1,0:T(8,128)(2,1)S(1)} fusion(bf16[1,128,512]{2,1,0:T(8,128)(2,1)} %param.18), kind=kLoop, calls=%fused_computation.3 | loop fusion | bytes 262144
  1.6 3.6 %collective-permute-start.8 = (bf16[2,128,512]{2,1,0:T(8,128)(2,1)S(1)}, bf16[2,128,512]{2,1,0:T(8,128)(2,1)S(1)}, u32[]{:S(2)}, u32[]{:S(2)}) collective-permute-start(bf16[2,128,512]{2,1,0:T(8,128)(2,1)S(1)} %constant_dynamic-update-slice_fusion.refs_6_.refs_7_), channel_id=1, source_target_pairs={{0,4},{1,5},{2,6},{3,7},{4,8},{5,9},{6,10},{7,11},{8,12},{9,13},{1... | collective-permute-start | bytes 786440 | tf_op jit(solution)/shard_map/ppermute | solution.py:20
  5.3 5.7 %collective-permute-start.11 = (bf16[2,128,512]{2,1,0:T(8,128)(2,1)S(1)}, bf16[2,128,512]{2,1,0:T(8,128)(2,1)S(1)}, u32[]{:S(2)}, u32[]{:S(2)}) collective-permute-start(bf16[2,128,512]{2,1,0:T(8,128)(2,1)S(1)} %constant_dynamic-update-slice_fusion.refs_6_.refs_7_), channel_id=1, source_target_pairs={{0,8},{1,9},{2,10},{3,11},{4,12},{5,13},{6,14},{7,15},{8,16},{9,17... | collective-permute-start | bytes 786440 | tf_op jit(solution)/shard_map/ppermute | solution.py:20
  11.0 4.9 %collective-permute-start.10 = (bf16[2,128,512]{2,1,0:T(8,128)(2,1)S(1)}, bf16[2,128,512]{2,1,0:T(8,128)(2,1)S(1)}, u32[]{:S(2)}, u32[]{:S(2)}) collective-permute-start(bf16[2,128,512]{2,1,0:T(8,128)(2,1)S(1)} %constant_dynamic-update-slice_fusion.refs_6_.refs_7_), channel_id=1, source_target_pairs={{0,2},{1,3},{2,4},{3,5},{4,6},{5,7},{6,8},{7,9},{8,10},{9,11},{10,... | collective-permute-start | bytes 786440 | tf_op jit(solution)/shard_map/ppermute | solution.py:20
  16.0 1.0 %collective-permute-done.8.refs_10_ = bf16[2,128,512]{2,1,0:T(8,128)(2,1)S(1)} collective-permute-done((bf16[2,128,512]{2,1,0:T(8,128)(2,1)S(1)}, bf16[2,128,512]{2,1,0:T(8,128)(2,1)S(1)}, u32[]{:S(2)}, u32[]{:S(2)}) %collective-permute-start.8) | collective-permute-done | bytes 262176 | tf_op jit(solution)/shard_map/ppermute | solution.py:20
  17.0 3.4 %collective-permute-start.9 = (bf16[2,128,512]{2,1,0:T(8,128)(2,1)S(1)}, bf16[2,128,512]{2,1,0:T(8,128)(2,1)S(1)}, u32[]{:S(2)}, u32[]{:S(2)}) collective-permute-start(bf16[2,128,512]{2,1,0:T(8,128)(2,1)S(1)} %broadcast_select_fusion), channel_id=1, source_target_pairs={{0,1},{1,2},{2,3},{3,0},{4,5},{5,6},{6,7},{7,4},{8,9},{9,10},{10,1... | collective-permute-start | bytes 786440 | tf_op jit(solution)/shard_map/ppermute | solution.py:26
  20.4 0.1 fusion.4
  20.5 0.1 copy.16
  20.5 0.1 copy.15
  20.6 0.6 copy-done.1
  21.2 0.7 fusion.2
  22.6 6.7 %conditional.2 = (bf16[2,128,512]{2,1,0:T(8,128)(2,1)}) conditional(s32[]{:T(128)} %clamp.4, () %tuple.39, bf16[2,128,512]{2,1,0:T(8,128)(2,1)S(1)} %constant_dynamic-update-slice_fusion.refs_6_.refs_7_, bf16[2,128,512]{2,1,0:T(8,128)(2,1)S(1)} %constant_dynamic-update-slice_fusion.refs_6_.refs_7_, ...), branch_computations={%region_1.2_spmd, %region_2.3_spmd, %region_3.4_spmd, %region_4.5_... | conditional | bytes 1048624 | solution.py:40
  22.6 3.5 %collective-permute-start.1 = (bf16[2,128,512]{2,1,0:T(8,128)(2,1)S(1)}, bf16[2,128,512]{2,1,0:T(8,128)(2,1)}, u32[]{:S(2)}, u32[]{:S(2)}) collective-permute-start(bf16[2,128,512]{2,1,0:T(8,128)(2,1)S(1)} %param.2), channel_id=1, source_target_pairs={{4,20},{5,21},{6,22},{7,23},{36,52},{37,53},{38,54},{39,55},{68,84... | collective-permute-start | bytes 786440 | tf_op jit(solution)/shard_map/cond/branch_2_fun/ppermute | solution.py:38
  26.1 3.2 %collective-permute-done.1 = bf16[2,128,512]{2,1,0:T(8,128)(2,1)} collective-permute-done((bf16[2,128,512]{2,1,0:T(8,128)(2,1)S(1)}, bf16[2,128,512]{2,1,0:T(8,128)(2,1)}, u32[]{:S(2)}, u32[]{:S(2)}) %collective-permute-start.1) | collective-permute-done | bytes 262176 | tf_op jit(solution)/shard_map/cond/branch_2_fun/ppermute | solution.py:38
  29.2 1.0 %prepare.1 = (f32[768,128]{1,0:T(8,128)S(1)}, bf16[2048,128]{1,0:T(8,128)(2,1)S(1)}, bf16[2048,128]{1,0:T(8,128)(2,1)S(1)}, f32[512,512]{1,0:T(8,128)S(1)}, f32[512,512]{1,0:T(8,128)S(1)}) custom-call(s32[1]{0:T(128)} %bitcast.refs_0_, s32[1,32]{1,0:T(1,128)S(1)} %copy-done.1, s32[1,4096]{1,0:T(1,128)S(1)} %copy-done, bf16[1,128,2048]{2,1,0:T(8,128)(2,1)S(1)} %copy-done.3, ...), custom_call_target="tpu_custom_call" | custom-call | flops 1000000000 | bytes 4000000 | tf_op jit(solution)/shard_map/prepare/pallas_call | solution.py:211
  30.3 0.7 collective-permute-done.9.refs_8_
  31.0 7.7 %attention_both_ways.1 = (bf16[1,128,2048]{2,1,0:T(8,128)(2,1)}, f32[2,128,512]{2,1,0:T(8,128)S(1)}, bf16[2,128,512]{2,1,0:T(8,128)(2,1)S(1)}, bf16[2,128,512]{2...) custom-call(bf16[1,128,2048]{2,1,0:T(8,128)(2,1)S(1)} %copy-done.3, ...), custom_call_target="tpu_custom_call" | custom-call | flops 2000000000 | bytes 6000000 | tf_op jit(solution)/shard_map/attention_both_ways/pallas_call | solution.py:227
  38.8 0.7 broadcast_in_dim.22
  39.5 11.3 %all-to-all-start = ((f32[32,16,128]{2,1,0:T(8,128)}), f32[32,16,128]{2,1,0:T(8,128)S(1)}, u32[]{:S(2)}, u32[]{:S(2)}) async-start(f32[32,16,128]{2,1,0:T(8,128)} %broadcast_in_dim.22), calls=%async_computation | async-start | bytes 524288 | tf_op jit(solution)/shard_map/all_to_all | solution.py:255
  50.8 4.6 %collective-permute-start.12 = (bf16[2,128,512]{2,1,0:T(8,128)(2,1)S(1)}, bf16[2,128,512]{2,1,0:T(8,128)(2,1)S(1)}, u32[]{:S(2)}, u32[]{:S(2)}) collective-permute-start(bf16[2,128,512]{2,1,0:T(8,128)(2,1)S(1)} %get-tuple-element.46), channel_id=1, source_target_pairs={{1,0},{2,1},{3,2},{4,3},{5,4},{6,5},{7,6},{8,7},{9,8},{10,9},{11,1... | collective-permute-start | bytes 786440 | tf_op jit(solution)/shard_map/ppermute | solution.py:20
  55.4 2.8 %collective-permute-start.13 = (bf16[2,128,512]{2,1,0:T(8,128)(2,1)S(1)}, bf16[2,128,512]{2,1,0:T(8,128)(2,1)S(1)}, u32[]{:S(2)}, u32[]{:S(2)}) collective-permute-start(bf16[2,128,512]{2,1,0:T(8,128)(2,1)S(1)} %get-tuple-element.47), channel_id=1, source_target_pairs={{2,0},{3,1},{4,2},{5,3},{6,4},{7,5},{8,6},{9,7},{10,8},{11,9},{12,... | collective-permute-start | bytes 786440 | tf_op jit(solution)/shard_map/ppermute | solution.py:20
  58.1 1.9 %collective-permute-start.14 = (bf16[2,128,512]{2,1,0:T(8,128)(2,1)S(1)}, bf16[2,128,512]{2,1,0:T(8,128)(2,1)S(1)}, u32[]{:S(2)}, u32[]{:S(2)}) collective-permute-start(bf16[2,128,512]{2,1,0:T(8,128)(2,1)S(1)} %get-tuple-element.48), channel_id=1, source_target_pairs={{4,0},{5,1},{6,2},{7,3},{8,4},{9,5},{10,6},{11,7},{12,8},{13,9},{1... | collective-permute-start | bytes 786440 | tf_op jit(solution)/shard_map/ppermute | solution.py:20
  60.1 1.3 %collective-permute-start.15 = (bf16[2,128,512]{2,1,0:T(8,128)(2,1)S(1)}, bf16[2,128,512]{2,1,0:T(8,128)(2,1)S(1)}, u32[]{:S(2)}, u32[]{:S(2)}) collective-permute-start(bf16[2,128,512]{2,1,0:T(8,128)(2,1)S(1)} %get-tuple-element.49), channel_id=1, source_target_pairs={{8,0},{9,1},{10,2},{11,3},{12,4},{13,5},{14,6},{15,7},{16,8},{17,9... | collective-permute-start | bytes 786440 | tf_op jit(solution)/shard_map/ppermute | solution.py:20
  62.1 0.7 broadcast_in_dim.24
  62.8 0.3 copy-done.6
  63.1 10.9 %all-to-all-start.1 = ((f32[16,16,128]{2,1,0:T(8,128)}), f32[16,16,128]{2,1,0:T(8,128)S(1)}, u32[]{:S(2)}, u32[]{:S(2)}) async-start(f32[16,16,128]{2,1,0:T(8,128)} %broadcast_in_dim.24), calls=%async_computation.1 | async-start | bytes 262144 | tf_op jit(solution)/shard_map/all_to_all | solution.py:46
  74.0 18.3 %conditional.3 = (bf16[2,128,512]{2,1,0:T(8,128)(2,1)}) conditional(s32[]{:T(128)} %clamp.4, () %tuple.40, bf16[2,128,512]{2,1,0:T(8,128)(2,1)S(1)} %copy-done.6, bf16[2,128,512]{2,1,0:T(8,128)(2,1)S(1)} %copy-done.6, bf16[2,128,512]{2,1,0:T(8,128)(2,1)S(1)} %copy-done.6, bf16[2,128,512]{2,1,0:T(8,128)(2,1)S(1)} %copy-done.6), branch_computations={%region_7.8_spmd, %region_8.9_spmd, %region_9.10_spmd, %region_10.... | conditional | bytes 1048624 | solution.py:40
  74.0 1.3 %collective-permute-start.5 = (bf16[2,128,512]{2,1,0:T(8,128)(2,1)S(1)}, bf16[2,128,512]{2,1,0:T(8,128)(2,1)}, u32[]{:S(2)}, u32[]{:S(2)}) collective-permute-start(bf16[2,128,512]{2,1,0:T(8,128)(2,1)S(1)} %param.7), channel_id=1, source_target_pairs={{20,4},{21,5},{22,6},{23,7},{52,36},{53,37},{54,38},{55,39},{84,68... | collective-permute-start | bytes 786440 | tf_op jit(solution)/shard_map/cond/branch_2_fun/ppermute | solution.py:38
  75.3 17.0 %collective-permute-done.5 = bf16[2,128,512]{2,1,0:T(8,128)(2,1)} collective-permute-done((bf16[2,128,512]{2,1,0:T(8,128)(2,1)S(1)}, bf16[2,128,512]{2,1,0:T(8,128)(2,1)}, u32[]{:S(2)}, u32[]{:S(2)}) %collective-permute-start.5) | collective-permute-done | bytes 262176 | tf_op jit(solution)/shard_map/cond/branch_2_fun/ppermute | solution.py:38
  92.2 1.2 %add_convert_fusion = bf16[2,128,512]{2,1,0:T(8,128)(2,1)S(1)} fusion(bf16[2,128,512]{2,1,0:T(8,128)(2,1)S(1)} %collective-permute-done.15, bf16[2,128,512]{2,1,0:T(8,128)(2,1)S(1)} %collective-permute-done.14, bf16[2,128,512]{2,1,0:T(8,128)(2,1)S(1)} %collective-permute-done.13, f32[2,128,512]{2,1,0:T(8,128)S(1)} %get-tuple-element.45, ...), kind=kLoop, calls=%fused_computation | loop fusion | flops 1572864 | bytes 2097153 | tf_op jit(solution)/shard_map/convert.1
  93.4 0.7 fusion.3
  94.1 0.6 reduce_sum.19
  (23 shorter events, 0.1 us)
Async XLA Ops:
  0.6 1.0 %copy-start.5 = (bf16[1,128,512]{2,1,0:T(8,128)(2,1)S(1)}, bf16[1,128,512]{2,1,0:T(8,128)(2,1)}, u32[]{:S(2)}) copy-start(bf16[1,128,512]{2,1,0:T(8,128)(2,1)} %param.19) | copy-start | bytes 393220
  1.6 27.6 %copy-start.3 = (bf16[1,128,2048]{2,1,0:T(8,128)(2,1)S(1)}, bf16[1,128,2048]{2,1,0:T(8,128)(2,1)}, u32[]{:S(2)}) copy-start(bf16[1,128,2048]{2,1,0:T(8,128)(2,1)} %refs_0_.1) | copy-start | bytes 1572868
  1.6 15.3 %collective-permute-start.8 = (bf16[2,128,512]{2,1,0:T(8,128)(2,1)S(1)}, bf16[2,128,512]{2,1,0:T(8,128)(2,1)S(1)}, u32[]{:S(2)}, u32[]{:S(2)}) collective-permute-start(bf16[2,128,512]{2,1,0:T(8,128)(2,1)S(1)} %constant_dynamic-update-slice_fusion.refs_6_.refs_7_), channel_id=1, source_target_pairs={{0,4},{1,5},{2,6},{3,7},{4,8},{5,9},{6,10},{7,11},{8,12},{9,13},{1... | collective-permute-start | bytes 786440 | tf_op jit(solution)/shard_map/ppermute | solution.py:20
  5.3 25.0 %collective-permute-start.11 = (bf16[2,128,512]{2,1,0:T(8,128)(2,1)S(1)}, bf16[2,128,512]{2,1,0:T(8,128)(2,1)S(1)}, u32[]{:S(2)}, u32[]{:S(2)}) collective-permute-start(bf16[2,128,512]{2,1,0:T(8,128)(2,1)S(1)} %constant_dynamic-update-slice_fusion.refs_6_.refs_7_), channel_id=1, source_target_pairs={{0,8},{1,9},{2,10},{3,11},{4,12},{5,13},{6,14},{7,15},{8,16},{9,17... | collective-permute-start | bytes 786440 | tf_op jit(solution)/shard_map/ppermute | solution.py:20
  11.0 19.3 %collective-permute-start.10 = (bf16[2,128,512]{2,1,0:T(8,128)(2,1)S(1)}, bf16[2,128,512]{2,1,0:T(8,128)(2,1)S(1)}, u32[]{:S(2)}, u32[]{:S(2)}) collective-permute-start(bf16[2,128,512]{2,1,0:T(8,128)(2,1)S(1)} %constant_dynamic-update-slice_fusion.refs_6_.refs_7_), channel_id=1, source_target_pairs={{0,2},{1,3},{2,4},{3,5},{4,6},{5,7},{6,8},{7,9},{8,10},{9,11},{10,... | collective-permute-start | bytes 786440 | tf_op jit(solution)/shard_map/ppermute | solution.py:20
  15.9 4.4 %copy-start = (s32[1,4096]{1,0:T(1,128)S(1)}, s32[1,4096]{1,0:T(1,128)}, u32[]{:S(2)}) copy-start(s32[1,4096]{1,0:T(1,128)} %refs_2_.1) | copy-start | bytes 49156
  16.0 13.3 %copy-start.2 = (bf16[1,128,2048]{2,1,0:T(8,128)(2,1)S(1)}, bf16[1,128,2048]{2,1,0:T(8,128)(2,1)}, u32[]{:S(2)}) copy-start(bf16[1,128,2048]{2,1,0:T(8,128)(2,1)} %refs_4_.1) | copy-start | bytes 1572868
  17.0 14.0 %collective-permute-start.9 = (bf16[2,128,512]{2,1,0:T(8,128)(2,1)S(1)}, bf16[2,128,512]{2,1,0:T(8,128)(2,1)S(1)}, u32[]{:S(2)}, u32[]{:S(2)}) collective-permute-start(bf16[2,128,512]{2,1,0:T(8,128)(2,1)S(1)} %broadcast_select_fusion), channel_id=1, source_target_pairs={{0,1},{1,2},{2,3},{3,0},{4,5},{5,6},{6,7},{7,4},{8,9},{9,10},{10,1... | collective-permute-start | bytes 786440 | tf_op jit(solution)/shard_map/ppermute | solution.py:26
  20.5 0.7 copy-start.1
  22.6 6.7 %copy-start.4 = (f32[16,128]{1,0:T(8,128)S(1)}, f32[16,128]{1,0:T(8,128)}, u32[]{:S(2)}) copy-start(f32[16,128]{1,0:T(8,128)} %refs_1_.3) | copy-start | bytes 24580
  22.6 6.6 %collective-permute-start.1 = (bf16[2,128,512]{2,1,0:T(8,128)(2,1)S(1)}, bf16[2,128,512]{2,1,0:T(8,128)(2,1)}, u32[]{:S(2)}, u32[]{:S(2)}) collective-permute-start(bf16[2,128,512]{2,1,0:T(8,128)(2,1)S(1)} %param.2), channel_id=1, source_target_pairs={{4,20},{5,21},{6,22},{7,23},{36,52},{37,53},{38,54},{39,55},{68,84... | collective-permute-start | bytes 786440 | tf_op jit(solution)/shard_map/cond/branch_2_fun/ppermute | solution.py:38
  39.5 22.5 %all-to-all-start = ((f32[32,16,128]{2,1,0:T(8,128)}), f32[32,16,128]{2,1,0:T(8,128)S(1)}, u32[]{:S(2)}, u32[]{:S(2)}) async-start(f32[32,16,128]{2,1,0:T(8,128)} %broadcast_in_dim.22), calls=%async_computation | async-start | bytes 524288 | tf_op jit(solution)/shard_map/all_to_all | solution.py:255
  50.8 41.4 %collective-permute-start.12 = (bf16[2,128,512]{2,1,0:T(8,128)(2,1)S(1)}, bf16[2,128,512]{2,1,0:T(8,128)(2,1)S(1)}, u32[]{:S(2)}, u32[]{:S(2)}) collective-permute-start(bf16[2,128,512]{2,1,0:T(8,128)(2,1)S(1)} %get-tuple-element.46), channel_id=1, source_target_pairs={{1,0},{2,1},{3,2},{4,3},{5,4},{6,5},{7,6},{8,7},{9,8},{10,9},{11,1... | collective-permute-start | bytes 786440 | tf_op jit(solution)/shard_map/ppermute | solution.py:20
  55.4 36.9 %collective-permute-start.13 = (bf16[2,128,512]{2,1,0:T(8,128)(2,1)S(1)}, bf16[2,128,512]{2,1,0:T(8,128)(2,1)S(1)}, u32[]{:S(2)}, u32[]{:S(2)}) collective-permute-start(bf16[2,128,512]{2,1,0:T(8,128)(2,1)S(1)} %get-tuple-element.47), channel_id=1, source_target_pairs={{2,0},{3,1},{4,2},{5,3},{6,4},{7,5},{8,6},{9,7},{10,8},{11,9},{12,... | collective-permute-start | bytes 786440 | tf_op jit(solution)/shard_map/ppermute | solution.py:20
  58.1 34.1 %collective-permute-start.14 = (bf16[2,128,512]{2,1,0:T(8,128)(2,1)S(1)}, bf16[2,128,512]{2,1,0:T(8,128)(2,1)S(1)}, u32[]{:S(2)}, u32[]{:S(2)}) collective-permute-start(bf16[2,128,512]{2,1,0:T(8,128)(2,1)S(1)} %get-tuple-element.48), channel_id=1, source_target_pairs={{4,0},{5,1},{6,2},{7,3},{8,4},{9,5},{10,6},{11,7},{12,8},{13,9},{1... | collective-permute-start | bytes 786440 | tf_op jit(solution)/shard_map/ppermute | solution.py:20
  60.1 32.2 %collective-permute-start.15 = (bf16[2,128,512]{2,1,0:T(8,128)(2,1)S(1)}, bf16[2,128,512]{2,1,0:T(8,128)(2,1)S(1)}, u32[]{:S(2)}, u32[]{:S(2)}) collective-permute-start(bf16[2,128,512]{2,1,0:T(8,128)(2,1)S(1)} %get-tuple-element.49), channel_id=1, source_target_pairs={{8,0},{9,1},{10,2},{11,3},{12,4},{13,5},{14,6},{15,7},{16,8},{17,9... | collective-permute-start | bytes 786440 | tf_op jit(solution)/shard_map/ppermute | solution.py:20
  62.1 1.0 %copy-start.6 = (bf16[2,128,512]{2,1,0:T(8,128)(2,1)S(1)}, bf16[2,128,512]{2,1,0:T(8,128)(2,1)}, u32[]{:S(2)}) copy-start(bf16[2,128,512]{2,1,0:T(8,128)(2,1)} %get-tuple-element.52) | copy-start | bytes 786436
  63.1 31.1 %all-to-all-start.1 = ((f32[16,16,128]{2,1,0:T(8,128)}), f32[16,16,128]{2,1,0:T(8,128)S(1)}, u32[]{:S(2)}, u32[]{:S(2)}) async-start(f32[16,16,128]{2,1,0:T(8,128)} %broadcast_in_dim.24), calls=%async_computation.1 | async-start | bytes 262144 | tf_op jit(solution)/shard_map/all_to_all | solution.py:46
  74.0 18.3 %collective-permute-start.5 = (bf16[2,128,512]{2,1,0:T(8,128)(2,1)S(1)}, bf16[2,128,512]{2,1,0:T(8,128)(2,1)}, u32[]{:S(2)}, u32[]{:S(2)}) collective-permute-start(bf16[2,128,512]{2,1,0:T(8,128)(2,1)S(1)} %param.7), channel_id=1, source_target_pairs={{20,4},{21,5},{22,6},{23,7},{52,36},{53,37},{54,38},{55,39},{84,68... | collective-permute-start | bytes 786440 | tf_op jit(solution)/shard_map/cond/branch_2_fun/ppermute | solution.py:38
